TPU v7x, 32 devices: a whole 2x2x4 slice. The times are simulated.
32 devices in a mesh: seq: 8 (over z, y), head: 4 (over x, core).
Axes of the slice: x: 2, y: 2, z: 4, core: 2. Of those that a mesh axis runs over, the one named last changes fastest.
Arguments:
- query_rows: bfloat16 [1024, 512], P('seq', 'head'), may hold values from -6 to 6
- key_rows: bfloat16 [1024, 512], P('seq', 'head'), may hold values from -6 to 6
- value_rows: bfloat16 [1024, 512], P('seq', 'head'), may hold values from -6 to 6
- gate_rows: bfloat16 [1024, 512], P('seq', 'head'), may hold values from -6 to 6
- cotangent: bfloat16 [1024, 512], P('seq', 'head'), may hold values from -6 to 6
- event_gaps: int32 [1024], P('seq'), may hold values from 0 to 7
- block_lists: int32 [8, 8], replicated, may hold values from -1 to 6, as said below
- bias_table: float32 [8, 16], P('head'), may hold values from -1 to 1
- norm_gain: float32 [512], P('head'), may hold values from 0.1 to 1.9
Outputs:
- layer_out: bfloat16 [1024, 512], P('seq', 'head')
- grad_query: bfloat16 [1024, 512], P('seq', 'head')
- grad_key: bfloat16 [1024, 512], P('seq', 'head')
- grad_value: bfloat16 [1024, 512], P('seq', 'head')
- grad_gate: bfloat16 [1024, 512], P('seq', 'head')
Inputs may be any that keep to these rules, and one draw needn't show every extreme that they name: `block_lists`: slot s of row c holds either c - 2**s or -1; it holds -1 wherever 2**s >= 8 or 2**s > c. The last row lists every group c - 2**s that exists.
All inputs are finite; a program needn't handle non-finite values.
Results may differ from a plain program's by a relative error of at most 0.01.
Values may be sent and summed in bfloat16 or wider, within the bound.
A program may use at most 64 MiB of HBM per device.

v0:
```python
import jax
import jax.numpy as jnp
from jax import lax
from jax.sharding import PartitionSpec as P

norm_eps = 1e-05


def prefix(x, axis, combine, identity):
    length, index = (lax.axis_size(axis), lax.axis_index(axis))
    everything = lax.all_gather(x, axis)
    start = jnp.broadcast_to(jnp.asarray(identity, x.dtype), x.shape)

    def step(k, before):
        reached = k < index
        new = combine(before, everything[k])
        return jnp.where(reached, new, before)

    return lax.fori_loop(0, length, step, start)


def shifted(x, axis, by):
    length = lax.axis_size(axis)
    pairs = [(i, i + by) for i in range(length) if 0 <= i + by < length]
    return lax.ppermute(x, axis, pairs)


def bucket_bias(delta, table):
    bias = jnp.zeros((table.shape[0],) + delta.shape, jnp.float32) + table[:, 0][:, None, None]
    for bucket_id in range(1, table.shape[1]):
        increment = (table[:, bucket_id] - table[:, bucket_id - 1])[:, None, None]
        reached = (delta >= 2 ** (bucket_id - 1)).astype(jnp.float32)
        bias = bias + increment * reached[None]
    return bias


def causal_mask(length):
    later_ids = lax.broadcasted_iota(jnp.int32, (length, length), 1)
    early_ids = lax.broadcasted_iota(jnp.int32, (length, length), 0)
    return (later_ids <= early_ids).astype(jnp.float32)


def add_counts(earlier, later):
    return earlier + later


def block_scores(query_heads, key_heads, query_times, key_times, table, scaling):
    scores = (
        jnp.einsum("qhd,khd->hqk", query_heads, key_heads, preferred_element_type=jnp.float32)
        * scaling
    )
    return scores + bucket_bias(query_times[:, None] - key_times[None, :], table)


def attend_block(
    running, query_heads, key_heads, value_heads, query_times, key_times, table, scaling, keep_mask
):
    weights = jax.nn.silu(
        block_scores(query_heads, key_heads, query_times, key_times, table, scaling)
    )
    if keep_mask is not None:
        weights = weights * keep_mask[None]
    weights = weights.astype(jnp.bfloat16)
    return running + jnp.einsum(
        "hqk,khd->qhd", weights, value_heads, preferred_element_type=jnp.float32
    )


def block_slopes(
    query_heads,
    key_heads,
    value_heads,
    grad_heads,
    query_times,
    key_times,
    table,
    scaling,
    keep_mask,
):
    scores = block_scores(query_heads, key_heads, query_times, key_times, table, scaling)
    sigmoid_val = jax.nn.sigmoid(scores)
    weights = jax.nn.silu(scores)
    slope = sigmoid_val * (1.0 + scores * (1.0 - sigmoid_val))
    grad_weights = jnp.einsum(
        "qhd,khd->hqk", grad_heads, value_heads, preferred_element_type=jnp.float32
    )
    grad_scores = grad_weights * slope
    if keep_mask is not None:
        weights = weights * keep_mask[None]
        grad_scores = grad_scores * keep_mask[None]
    return (weights.astype(jnp.bfloat16), grad_scores.astype(jnp.bfloat16))


def skip_block(running):
    return running


def per_device(
    query_rows,
    key_rows,
    value_rows,
    gate_rows,
    cotangent,
    event_gaps,
    block_lists,
    bias_table,
    norm_gain,
):
    row_count = query_rows.shape[0]
    feature_dim = query_rows.shape[1]
    head_count = bias_table.shape[0]
    head_dim = feature_dim // head_count
    scaling = head_dim ** (-0.5)
    full_width = feature_dim * lax.axis_size("head")
    seq_count = lax.axis_size("seq")
    group_id = lax.axis_index("seq")

    def split_heads(flat_rows):
        return flat_rows.reshape(flat_rows.shape[0], head_count, head_dim)

    local_times = jnp.cumsum(event_gaps)
    before = prefix(local_times[-1], "seq", add_counts, jnp.int32(0))
    event_times = local_times + before
    query_heads = split_heads(query_rows)
    key_heads = split_heads(key_rows)
    value_heads = split_heads(value_rows)
    diagonal = causal_mask(row_count)
    my_entries = lax.dynamic_index_in_dim(block_lists, group_id, 0, keepdims=False)
    offsets = [
        (slot_id, 2**slot_id) for slot_id in range(block_lists.shape[1]) if 2**slot_id < seq_count
    ]
    attended = attend_block(
        jnp.zeros(query_heads.shape, jnp.float32),
        query_heads,
        key_heads,
        value_heads,
        event_times,
        event_times,
        bias_table,
        scaling,
        diagonal,
    )
    kept = []
    for slot_id, distance in offsets:
        fetched = shifted((key_rows, value_rows, event_times), "seq", distance)
        kept.append(fetched)

        def add_remote(running, fetched=fetched):
            return attend_block(
                running,
                query_heads,
                split_heads(fetched[0]),
                split_heads(fetched[1]),
                event_times,
                fetched[2],
                bias_table,
                scaling,
                None,
            )

        attended = lax.cond(my_entries[slot_id] >= 0, add_remote, skip_block, attended)
    flat = attended.reshape(row_count, feature_dim)
    norm_sums = lax.psum((jnp.sum(flat, axis=1), jnp.sum(flat * flat, axis=1)), "head")
    row_mean = norm_sums[0] / full_width
    row_var = norm_sums[1] / full_width - row_mean * row_mean
    inv_std = lax.rsqrt(row_var + norm_eps)
    centered = (flat - row_mean[:, None]) * inv_std[:, None]
    normed = centered * norm_gain[None, :]
    gates = gate_rows.astype(jnp.float32)
    upstream = cotangent.astype(jnp.float32)
    layer_out = (normed * gates).astype(jnp.bfloat16)
    grad_gate = (upstream * normed).astype(jnp.bfloat16)
    scaled = upstream * gates * norm_gain[None, :]
    grad_sums = lax.psum((jnp.sum(scaled, axis=1), jnp.sum(scaled * centered, axis=1)), "head")
    grad_attended = inv_std[:, None] * (
        scaled - grad_sums[0][:, None] / full_width - centered * grad_sums[1][:, None] / full_width
    )
    grad_flat = grad_attended.astype(jnp.bfloat16)
    grad_heads = split_heads(grad_flat)
    weights, grad_scores = block_slopes(
        query_heads,
        key_heads,
        value_heads,
        grad_heads,
        event_times,
        event_times,
        bias_table,
        scaling,
        diagonal,
    )
    grad_query = (
        jnp.einsum("hqk,khd->qhd", grad_scores, key_heads, preferred_element_type=jnp.float32)
        * scaling
    )
    key_grad = (
        jnp.einsum("hqk,qhd->khd", grad_scores, query_heads, preferred_element_type=jnp.float32)
        * scaling
    )
    value_grad = jnp.einsum("hqk,qhd->khd", weights, grad_heads, preferred_element_type=jnp.float32)
    empty_heads = jnp.zeros(query_heads.shape, jnp.float32)
    for position, (slot_id, distance) in enumerate(offsets):
        fetched = kept[position]
        listed = my_entries[slot_id] >= 0
        remote_keys = split_heads(fetched[0])
        remote_values = split_heads(fetched[1])
        remote_times = fetched[2]

        def remote_grads(
            unused, remote_keys=remote_keys, remote_values=remote_values, remote_times=remote_times
        ):
            block_weights, block_grads = block_slopes(
                query_heads,
                remote_keys,
                remote_values,
                grad_heads,
                event_times,
                remote_times,
                bias_table,
                scaling,
                None,
            )
            query_part = (
                jnp.einsum(
                    "hqk,khd->qhd", block_grads, remote_keys, preferred_element_type=jnp.float32
                )
                * scaling
            )
            key_part = (
                jnp.einsum(
                    "hqk,qhd->khd", block_grads, query_heads, preferred_element_type=jnp.float32
                )
                * scaling
            )
            value_part = jnp.einsum(
                "hqk,qhd->khd", block_weights, grad_heads, preferred_element_type=jnp.float32
            )
            return (query_part, key_part, value_part)

        def no_grads(unused):
            return (empty_heads, empty_heads, empty_heads)

        query_part, key_part, value_part = lax.cond(listed, remote_grads, no_grads, jnp.int32(0))
        grad_query = grad_query + query_part
        returned = (
            shifted(key_part.astype(jnp.bfloat16), "seq", -distance).astype(key_part.dtype),
            shifted(value_part.astype(jnp.bfloat16), "seq", -distance).astype(value_part.dtype),
        )
        key_grad = key_grad + returned[0]
        value_grad = value_grad + returned[1]
    grad_query_out = grad_query.reshape(row_count, feature_dim).astype(jnp.bfloat16)
    grad_key_out = key_grad.reshape(row_count, feature_dim).astype(jnp.bfloat16)
    grad_value_out = value_grad.reshape(row_count, feature_dim).astype(jnp.bfloat16)
    return (layer_out, grad_query_out, grad_key_out, grad_value_out, grad_gate)


def solution(mesh):
    placed = (
        P("seq", "head"),
        P("seq", "head"),
        P("seq", "head"),
        P("seq", "head"),
        P("seq", "head"),
        P("seq"),
        P(),
        P("head", None),
        P("head"),
    )
    return jax.shard_map(
        per_device,
        mesh=mesh,
        in_specs=placed,
        out_specs=(
            P("seq", "head"),
            P("seq", "head"),
            P("seq", "head"),
            P("seq", "head"),
            P("seq", "head"),
        ),
        check_vma=False,
    )
```

profile of v0, /device:TPU:0, one launch (start us, length us, event | category | flops | bytes accessed | tf_op | source)
XLA Modules:
  0.0 96.8 jit_solution(13662373353368392941)
XLA Ops:
  0.6 0.9 copy.44
  1.5 5.9 %collective-permute-start.8 = (bf16[128,128]{0,1:T(8,128)(2,1)S(1)}, bf16[128,128]{0,1:T(8,128)(2,1)S(1)}, u32[]{:S(2)}, u32[]{:S(2)}) collective-permute-start(bf16[128,128]{0,1:T(8,128)(2,1)S(1)} %copy.44), channel_id=1, source_target_pairs={{0,16},{4,20},{8,24},{12,28},{1,17},{5,21},{9,25},{13,29},{2,18},{... | collective-permute-start | bytes 98312 | tf_op jit(solution)/shard_map/ppermute | solution.py:25
  7.5 3.5 %collective-permute-start.5 = (bf16[128,128]{0,1:T(8,128)(2,1)S(1)}, bf16[128,128]{0,1:T(8,128)(2,1)S(1)}, u32[]{:S(2)}, u32[]{:S(2)}) collective-permute-start(bf16[128,128]{0,1:T(8,128)(2,1)S(1)} %copy.44), channel_id=1, source_target_pairs={{0,8},{4,12},{8,16},{12,20},{16,24},{20,28},{1,9},{5,13},{9,17},{1... | collective-permute-start | bytes 98312 | tf_op jit(solution)/shard_map/ppermute | solution.py:25
  11.0 3.4 %collective-permute-start.2 = (bf16[128,128]{0,1:T(8,128)(2,1)S(1)}, bf16[128,128]{0,1:T(8,128)(2,1)S(1)}, u32[]{:S(2)}, u32[]{:S(2)}) collective-permute-start(bf16[128,128]{0,1:T(8,128)(2,1)S(1)} %copy.44), channel_id=1, source_target_pairs={{0,4},{4,8},{8,12},{12,16},{16,20},{20,24},{24,28},{1,5},{5,9},{9,... | collective-permute-start | bytes 98312 | tf_op jit(solution)/shard_map/ppermute | solution.py:25
  14.4 0.6 copy-done.7
  15.3 0.5 slice.610
  15.9 0.7 copy-done.8
  16.5 0.6 dynamic-slice
  17.1 1.3 %bitcast_dynamic-update-slice_fusion = s32[8]{0:T(128)S(1)} fusion(s32[8]{0:T(128)S(1)} %broadcast.2624, u32[]{:T(128)} %bitcast.128, s32[1,1]{1,0:T(1,128)} %slice.610), kind=kLoop, calls=%fused_computation.689 | loop fusion | bytes 40
  18.4 7.2 %all-reduce = s32[8]{0:T(128)S(1)} all-reduce(s32[8]{0:T(128)S(1)} %bitcast_dynamic-update-slice_fusion), channel_id=2, replica_groups=mesh['seq'=8,'head'=4] {'seq'}, use_global_device_ids=true, to_apply=%add | all-reduce | flops 8 | bytes 64 | tf_op jit(solution)/shard_map/all_gather | solution.py:11
  25.6 10.1 %while.13 = (s32[]{:T(128)}, s32[]{:T(128)}, s32[]{:T(128)}, s32[8]{0:T(128)S(1)}, s32[]{:T(128)}) while((s32[]{:T(128)}, s32[]{:T(128)}, s32[]{:T(128)}, s32[8]{0:T(128)S(1)}, s32[]{:T(128)}) %tuple.310), condition=%wide.region_2.3_spmd, body=%wide.region_1.2_spmd.sunk | while | flops 5 | bytes 115 | solution.py:19
  25.6 0.6 dynamic_slice.14
  26.9 0.6 dynamic_slice.14
  28.2 0.6 dynamic_slice.14
  29.4 0.6 dynamic_slice.14
  30.7 0.6 dynamic_slice.14
  32.0 0.6 dynamic_slice.14
  33.2 0.6 dynamic_slice.14
  34.5 0.6 dynamic_slice.14
  35.9 3.9 %collective-permute-start.4 = (s32[128]{0:T(128)S(1)}, s32[128]{0:T(128)S(1)}, u32[]{:S(2)}, u32[]{:S(2)}) collective-permute-start(s32[128]{0:T(128)S(1)} %add_reduce_fusion), channel_id=1, source_target_pairs={{0,8},{4,12},{8,16},{12,20},{16,24},{20,28},{1,9},{5,13},{9,17},{1... | collective-permute-start | bytes 1544 | tf_op jit(solution)/shard_map/ppermute | solution.py:25
  39.8 1.9 %collective-permute-start.1 = (s32[128]{0:T(128)S(1)}, s32[128]{0:T(128)S(1)}, u32[]{:S(2)}, u32[]{:S(2)}) collective-permute-start(s32[128]{0:T(128)S(1)} %add_reduce_fusion), channel_id=1, source_target_pairs={{0,4},{4,8},{8,12},{12,16},{16,20},{20,24},{24,28},{1,5},{5,9},{9,... | collective-permute-start | bytes 1544 | tf_op jit(solution)/shard_map/ppermute | solution.py:25
  41.9 0.7 copy-done.1
  42.6 0.4 slice_reduce_fusion.15
  43.2 0.6 copy-done.3
  44.0 0.3 multiply_convert_fusion.9
  44.5 5.1 %collective-permute-start.6 = (bf16[128,128]{0,1:T(8,128)(2,1)S(1)}, bf16[128,128]{0,1:T(8,128)(2,1)S(1)}, u32[]{:S(2)}, u32[]{:S(2)}) collective-permute-start(bf16[128,128]{0,1:T(8,128)(2,1)S(1)} %copy.42), channel_id=1, source_target_pairs={{0,16},{4,20},{8,24},{12,28},{1,17},{5,21},{9,25},{13,29},{2,18},{... | collective-permute-start | bytes 98312 | tf_op jit(solution)/shard_map/ppermute | solution.py:25
  49.6 1.3 %collective-permute-start.3 = (bf16[128,128]{0,1:T(8,128)(2,1)S(1)}, bf16[128,128]{0,1:T(8,128)(2,1)S(1)}, u32[]{:S(2)}, u32[]{:S(2)}) collective-permute-start(bf16[128,128]{0,1:T(8,128)(2,1)S(1)} %copy.42), channel_id=1, source_target_pairs={{0,8},{4,12},{8,16},{12,20},{16,24},{20,28},{1,9},{5,13},{9,17},{1... | collective-permute-start | bytes 98312 | tf_op jit(solution)/shard_map/ppermute | solution.py:25
  50.9 3.9 %collective-permute-start = (bf16[128,128]{0,1:T(8,128)(2,1)S(1)}, bf16[128,128]{0,1:T(8,128)(2,1)S(1)}, u32[]{:S(2)}, u32[]{:S(2)}) collective-permute-start(bf16[128,128]{0,1:T(8,128)(2,1)S(1)} %copy.42), channel_id=1, source_target_pairs={{0,4},{4,8},{8,12},{12,16},{16,20},{20,24},{24,28},{1,5},{5,9},{9,... | collective-permute-start | bytes 98312 | tf_op jit(solution)/shard_map/ppermute | solution.py:25
  54.8 0.6 fusion.424
  57.5 2.4 %collective-permute-start.7 = (s32[128]{0:T(128)S(1)}, s32[128]{0:T(128)S(1)}, u32[]{:S(2)}, u32[]{:S(2)}) collective-permute-start(s32[128]{0:T(128)S(1)} %add_reduce_fusion), channel_id=1, source_target_pairs={{0,16},{4,20},{8,24},{12,28},{1,17},{5,21},{9,25},{13,29},{2,18},{... | collective-permute-start | bytes 1544 | tf_op jit(solution)/shard_map/ppermute | solution.py:25
  60.1 1.1 %collective-permute-done.7 = s32[128]{0:T(128)S(1)} collective-permute-done((s32[128]{0:T(128)S(1)}, s32[128]{0:T(128)S(1)}, u32[]{:S(2)}, u32[]{:S(2)}) %collective-permute-start.7) | collective-permute-done | bytes 544 | tf_op jit(solution)/shard_map/ppermute | solution.py:25
  61.2 5.7 %all-reduce.2 = (f32[128]{0:T(128)S(1)}, f32[128]{0:T(128)S(1)}) all-reduce(f32[128]{0:T(128)S(1)} %get-tuple-element.344, f32[128]{0:T(128)S(1)} %get-tuple-element.343), channel_id=1, replica_groups=mesh['seq'=8,'head'=4] {'head'}, use_global_device_ids=true, to_apply=%region_12.13 | all-reduce | flops 256 | bytes 2048 | tf_op jit(solution)/shard_map/psum | solution.py:163
  66.9 0.7 copy-done.6
  67.7 6.6 %all-reduce.1 = (f32[128]{0:T(128)S(1)}, f32[128]{0:T(128)S(1)}) all-reduce(f32[128]{0:T(128)S(1)} %get-tuple-element.342, f32[128]{0:T(128)S(1)} %get-tuple-element.341), channel_id=1, replica_groups=mesh['seq'=8,'head'=4] {'head'}, use_global_device_ids=true, to_apply=%region_16.17 | all-reduce | flops 256 | bytes 2048 | tf_op jit(solution)/shard_map/psum | solution.py:174
  75.0 0.7 copy.63
  75.8 0.7 copy.59
  76.6 1.3 %collective-permute-start.12 = (bf16[128,2,64]{0,2,1:T(8,128)(2,1)S(1)}, bf16[128,2,64]{0,2,1:T(8,128)(2,1)S(1)}, u32[]{:S(2)}, u32[]{:S(2)}) collective-permute-start(bf16[128,2,64]{0,2,1:T(8,128)(2,1)S(1)} %convert_element_type.921), channel_id=1, source_target_pairs={{4,0},{8,4},{12,8},{16,12},{20,16},{24,20},{28,24},{5,1},{9,5},{13... | collective-permute-start | bytes 98312 | tf_op jit(solution)/shard_map/ppermute | solution.py:25
  77.9 1.3 %collective-permute-start.9 = (bf16[128,2,64]{0,2,1:T(8,128)(2,1)S(1)}, bf16[128,2,64]{0,2,1:T(8,128)(2,1)S(1)}, u32[]{:S(2)}, u32[]{:S(2)}) collective-permute-start(bf16[128,2,64]{0,2,1:T(8,128)(2,1)S(1)} %convert_element_type.913), channel_id=1, source_target_pairs={{4,0},{8,4},{12,8},{16,12},{20,16},{24,20},{28,24},{5,1},{9,5},{13... | collective-permute-start | bytes 98312 | tf_op jit(solution)/shard_map/ppermute | solution.py:25
  79.3 1.3 %collective-permute-start.13 = (bf16[128,2,64]{0,2,1:T(8,128)(2,1)S(1)}, bf16[128,2,64]{0,2,1:T(8,128)(2,1)S(1)}, u32[]{:S(2)}, u32[]{:S(2)}) collective-permute-start(bf16[128,2,64]{0,2,1:T(8,128)(2,1)S(1)} %convert_element_type.923), channel_id=1, source_target_pairs={{8,0},{12,4},{16,8},{20,12},{24,16},{28,20},{9,1},{13,5},{17,9},{2... | collective-permute-start | bytes 98312 | tf_op jit(solution)/shard_map/ppermute | solution.py:25
  80.6 1.3 %collective-permute-start.10 = (bf16[128,2,64]{0,2,1:T(8,128)(2,1)S(1)}, bf16[128,2,64]{0,2,1:T(8,128)(2,1)S(1)}, u32[]{:S(2)}, u32[]{:S(2)}) collective-permute-start(bf16[128,2,64]{0,2,1:T(8,128)(2,1)S(1)} %convert_element_type.915), channel_id=1, source_target_pairs={{8,0},{12,4},{16,8},{20,12},{24,16},{28,20},{9,1},{13,5},{17,9},{2... | collective-permute-start | bytes 98312 | tf_op jit(solution)/shard_map/ppermute | solution.py:25
  81.9 1.3 %collective-permute-start.14 = (bf16[128,2,64]{0,2,1:T(8,128)(2,1)S(1)}, bf16[128,2,64]{0,2,1:T(8,128)(2,1)S(1)}, u32[]{:S(2)}, u32[]{:S(2)}) collective-permute-start(bf16[128,2,64]{0,2,1:T(8,128)(2,1)S(1)} %convert_element_type.925), channel_id=1, source_target_pairs={{16,0},{20,4},{24,8},{28,12},{17,1},{21,5},{25,9},{29,13},{18,2},{... | collective-permute-start | bytes 98312 | tf_op jit(solution)/shard_map/ppermute | solution.py:25
  83.3 0.7 copy.60
  84.0 1.3 %collective-permute-start.11 = (bf16[128,2,64]{0,2,1:T(8,128)(2,1)S(1)}, bf16[128,2,64]{0,2,1:T(8,128)(2,1)S(1)}, u32[]{:S(2)}, u32[]{:S(2)}) collective-permute-start(bf16[128,2,64]{0,2,1:T(8,128)(2,1)S(1)} %convert_element_type.917), channel_id=1, source_target_pairs={{16,0},{20,4},{24,8},{28,12},{17,1},{21,5},{25,9},{29,13},{18,2},{... | collective-permute-start | bytes 98312 | tf_op jit(solution)/shard_map/ppermute | solution.py:25
  85.3 3.7 %collective-permute-done.13 = bf16[128,2,64]{0,2,1:T(8,128)(2,1)S(1)} collective-permute-done((bf16[128,2,64]{0,2,1:T(8,128)(2,1)S(1)}, bf16[128,2,64]{0,2,1:T(8,128)(2,1)S(1)}, u32[]{:S(2)}, u32[]{:S(2)}) %collective-permute-start.13) | collective-permute-done | bytes 32800 | tf_op jit(solution)/shard_map/ppermute | solution.py:25
  89.0 5.0 %collective-permute-done.14 = bf16[128,2,64]{0,2,1:T(8,128)(2,1)S(1)} collective-permute-done((bf16[128,2,64]{0,2,1:T(8,128)(2,1)S(1)}, bf16[128,2,64]{0,2,1:T(8,128)(2,1)S(1)}, u32[]{:S(2)}, u32[]{:S(2)}) %collective-permute-start.14) | collective-permute-done | bytes 32800 | tf_op jit(solution)/shard_map/ppermute | solution.py:25
  94.0 0.7 copy.62
  94.8 1.3 %collective-permute-done.11 = bf16[128,2,64]{0,2,1:T(8,128)(2,1)S(1)} collective-permute-done((bf16[128,2,64]{0,2,1:T(8,128)(2,1)S(1)}, bf16[128,2,64]{0,2,1:T(8,128)(2,1)S(1)}, u32[]{:S(2)}, u32[]{:S(2)}) %collective-permute-start.11) | collective-permute-done | bytes 32800 | tf_op jit(solution)/shard_map/ppermute | solution.py:25
  96.1 0.7 copy.61
  (70 shorter events, 2.5 us)
Async XLA Ops:
  0.6 43.8 %copy-start = (s32[8,8]{1,0:T(8,128)S(1)}, s32[8,8]{1,0:T(8,128)}, u32[]{:S(2)}) copy-start(s32[8,8]{1,0:T(8,128)} %param.29) | copy-start | bytes 772
  1.5 59.7 %collective-permute-start.8 = (bf16[128,128]{0,1:T(8,128)(2,1)S(1)}, bf16[128,128]{0,1:T(8,128)(2,1)S(1)}, u32[]{:S(2)}, u32[]{:S(2)}) collective-permute-start(bf16[128,128]{0,1:T(8,128)(2,1)S(1)} %copy.44), channel_id=1, source_target_pairs={{0,16},{4,20},{8,24},{12,28},{1,17},{5,21},{9,25},{13,29},{2,18},{... | collective-permute-start | bytes 98312 | tf_op jit(solution)/shard_map/ppermute | solution.py:25
  7.5 52.6 %collective-permute-start.5 = (bf16[128,128]{0,1:T(8,128)(2,1)S(1)}, bf16[128,128]{0,1:T(8,128)(2,1)S(1)}, u32[]{:S(2)}, u32[]{:S(2)}) collective-permute-start(bf16[128,128]{0,1:T(8,128)(2,1)S(1)} %copy.44), channel_id=1, source_target_pairs={{0,8},{4,12},{8,16},{12,20},{16,24},{20,28},{1,9},{5,13},{9,17},{1... | collective-permute-start | bytes 98312 | tf_op jit(solution)/shard_map/ppermute | solution.py:25
  11.0 40.0 %collective-permute-start.2 = (bf16[128,128]{0,1:T(8,128)(2,1)S(1)}, bf16[128,128]{0,1:T(8,128)(2,1)S(1)}, u32[]{:S(2)}, u32[]{:S(2)}) collective-permute-start(bf16[128,128]{0,1:T(8,128)(2,1)S(1)} %copy.44), channel_id=1, source_target_pairs={{0,4},{4,8},{8,12},{12,16},{16,20},{20,24},{24,28},{1,5},{5,9},{9,... | collective-permute-start | bytes 98312 | tf_op jit(solution)/shard_map/ppermute | solution.py:25
  14.4 0.7 copy-start.7
  15.9 0.7 copy-start.8
  35.9 8.6 %collective-permute-start.4 = (s32[128]{0:T(128)S(1)}, s32[128]{0:T(128)S(1)}, u32[]{:S(2)}, u32[]{:S(2)}) collective-permute-start(s32[128]{0:T(128)S(1)} %add_reduce_fusion), channel_id=1, source_target_pairs={{0,8},{4,12},{8,16},{12,20},{16,24},{20,28},{1,9},{5,13},{9,17},{1... | collective-permute-start | bytes 1544 | tf_op jit(solution)/shard_map/ppermute | solution.py:25
  39.8 9.8 %collective-permute-start.1 = (s32[128]{0:T(128)S(1)}, s32[128]{0:T(128)S(1)}, u32[]{:S(2)}, u32[]{:S(2)}) collective-permute-start(s32[128]{0:T(128)S(1)} %add_reduce_fusion), channel_id=1, source_target_pairs={{0,4},{4,8},{8,12},{12,16},{16,20},{20,24},{24,28},{1,5},{5,9},{9,... | collective-permute-start | bytes 1544 | tf_op jit(solution)/shard_map/ppermute | solution.py:25
  41.7 1.3 %copy-start.2 = (bf16[128,128]{1,0:T(8,128)(2,1)S(1)}, bf16[128,128]{1,0:T(8,128)(2,1)}, u32[]{:S(2)}) copy-start(bf16[128,128]{1,0:T(8,128)(2,1)} %param.24) | copy-start | bytes 98308
  41.9 0.7 copy-start.1
  43.0 0.8 copy-start.3
  44.3 13.1 %copy-start.4 = (bf16[128,128]{1,0:T(8,128)(2,1)S(1)}, bf16[128,128]{1,0:T(8,128)(2,1)}, u32[]{:S(2)}) copy-start(bf16[128,128]{1,0:T(8,128)(2,1)} %param.26) | copy-start | bytes 98308
  44.5 16.7 %collective-permute-start.6 = (bf16[128,128]{0,1:T(8,128)(2,1)S(1)}, bf16[128,128]{0,1:T(8,128)(2,1)S(1)}, u32[]{:S(2)}, u32[]{:S(2)}) collective-permute-start(bf16[128,128]{0,1:T(8,128)(2,1)S(1)} %copy.42), channel_id=1, source_target_pairs={{0,16},{4,20},{8,24},{12,28},{1,17},{5,21},{9,25},{13,29},{2,18},{... | collective-permute-start | bytes 98312 | tf_op jit(solution)/shard_map/ppermute | solution.py:25
  49.6 10.4 %collective-permute-start.3 = (bf16[128,128]{0,1:T(8,128)(2,1)S(1)}, bf16[128,128]{0,1:T(8,128)(2,1)S(1)}, u32[]{:S(2)}, u32[]{:S(2)}) collective-permute-start(bf16[128,128]{0,1:T(8,128)(2,1)S(1)} %copy.42), channel_id=1, source_target_pairs={{0,8},{4,12},{8,16},{12,20},{16,24},{20,28},{1,9},{5,13},{9,17},{1... | collective-permute-start | bytes 98312 | tf_op jit(solution)/shard_map/ppermute | solution.py:25
  50.9 6.6 %collective-permute-start = (bf16[128,128]{0,1:T(8,128)(2,1)S(1)}, bf16[128,128]{0,1:T(8,128)(2,1)S(1)}, u32[]{:S(2)}, u32[]{:S(2)}) collective-permute-start(bf16[128,128]{0,1:T(8,128)(2,1)S(1)} %copy.42), channel_id=1, source_target_pairs={{0,4},{4,8},{8,12},{12,16},{16,20},{20,24},{24,28},{1,5},{5,9},{9,... | collective-permute-start | bytes 98312 | tf_op jit(solution)/shard_map/ppermute | solution.py:25
  57.4 2.5 %copy-start.5 = (bf16[128,128]{1,0:T(8,128)(2,1)S(1)}, bf16[128,128]{1,0:T(8,128)(2,1)}, u32[]{:S(2)}) copy-start(bf16[128,128]{1,0:T(8,128)(2,1)} %param.27) | copy-start | bytes 98308
  57.5 3.7 %collective-permute-start.7 = (s32[128]{0:T(128)S(1)}, s32[128]{0:T(128)S(1)}, u32[]{:S(2)}, u32[]{:S(2)}) collective-permute-start(s32[128]{0:T(128)S(1)} %add_reduce_fusion), channel_id=1, source_target_pairs={{0,16},{4,20},{8,24},{12,28},{1,17},{5,21},{9,25},{13,29},{2,18},{... | collective-permute-start | bytes 1544 | tf_op jit(solution)/shard_map/ppermute | solution.py:25
  66.9 0.7 copy-start.6
  76.6 7.4 %collective-permute-start.12 = (bf16[128,2,64]{0,2,1:T(8,128)(2,1)S(1)}, bf16[128,2,64]{0,2,1:T(8,128)(2,1)S(1)}, u32[]{:S(2)}, u32[]{:S(2)}) collective-permute-start(bf16[128,2,64]{0,2,1:T(8,128)(2,1)S(1)} %convert_element_type.921), channel_id=1, source_target_pairs={{4,0},{8,4},{12,8},{16,12},{20,16},{24,20},{28,24},{5,1},{9,5},{13... | collective-permute-start | bytes 98312 | tf_op jit(solution)/shard_map/ppermute | solution.py:25
  77.9 16.9 %collective-permute-start.9 = (bf16[128,2,64]{0,2,1:T(8,128)(2,1)S(1)}, bf16[128,2,64]{0,2,1:T(8,128)(2,1)S(1)}, u32[]{:S(2)}, u32[]{:S(2)}) collective-permute-start(bf16[128,2,64]{0,2,1:T(8,128)(2,1)S(1)} %convert_element_type.913), channel_id=1, source_target_pairs={{4,0},{8,4},{12,8},{16,12},{20,16},{24,20},{28,24},{5,1},{9,5},{13... | collective-permute-start | bytes 98312 | tf_op jit(solution)/shard_map/ppermute | solution.py:25
  79.3 9.8 %collective-permute-start.13 = (bf16[128,2,64]{0,2,1:T(8,128)(2,1)S(1)}, bf16[128,2,64]{0,2,1:T(8,128)(2,1)S(1)}, u32[]{:S(2)}, u32[]{:S(2)}) collective-permute-start(bf16[128,2,64]{0,2,1:T(8,128)(2,1)S(1)} %convert_element_type.923), channel_id=1, source_target_pairs={{8,0},{12,4},{16,8},{20,12},{24,16},{28,20},{9,1},{13,5},{17,9},{2... | collective-permute-start | bytes 98312 | tf_op jit(solution)/shard_map/ppermute | solution.py:25
  80.6 14.2 %collective-permute-start.10 = (bf16[128,2,64]{0,2,1:T(8,128)(2,1)S(1)}, bf16[128,2,64]{0,2,1:T(8,128)(2,1)S(1)}, u32[]{:S(2)}, u32[]{:S(2)}) collective-permute-start(bf16[128,2,64]{0,2,1:T(8,128)(2,1)S(1)} %convert_element_type.915), channel_id=1, source_target_pairs={{8,0},{12,4},{16,8},{20,12},{24,16},{28,20},{9,1},{13,5},{17,9},{2... | collective-permute-start | bytes 98312 | tf_op jit(solution)/shard_map/ppermute | solution.py:25
  81.9 12.1 %collective-permute-start.14 = (bf16[128,2,64]{0,2,1:T(8,128)(2,1)S(1)}, bf16[128,2,64]{0,2,1:T(8,128)(2,1)S(1)}, u32[]{:S(2)}, u32[]{:S(2)}) collective-permute-start(bf16[128,2,64]{0,2,1:T(8,128)(2,1)S(1)} %convert_element_type.925), channel_id=1, source_target_pairs={{16,0},{20,4},{24,8},{28,12},{17,1},{21,5},{25,9},{29,13},{18,2},{... | collective-permute-start | bytes 98312 | tf_op jit(solution)/shard_map/ppermute | solution.py:25
  84.0 12.1 %collective-permute-start.11 = (bf16[128,2,64]{0,2,1:T(8,128)(2,1)S(1)}, bf16[128,2,64]{0,2,1:T(8,128)(2,1)S(1)}, u32[]{:S(2)}, u32[]{:S(2)}) collective-permute-start(bf16[128,2,64]{0,2,1:T(8,128)(2,1)S(1)} %convert_element_type.917), channel_id=1, source_target_pairs={{16,0},{20,4},{24,8},{28,12},{17,1},{21,5},{25,9},{29,13},{18,2},{... | collective-permute-start | bytes 98312 | tf_op jit(solution)/shard_map/ppermute | solution.py:25
where the time goes:
time: 97.1 us; the launch traced here: 96.8 us
  starting transfers between devices  39.1 us (40%)
  blocking collectives  19.5 us (20%)
  local copies, waits for them, and re-layouts  16.5 us (17%)
  waiting for transfers between devices  11.1 us (11%)
  loops' own time  5.53 us (6%)
  between operations  3.04 us (3%)
  matrix products  1.12 us (1%)
    ppermute x15, starting transfers between devices, shifted(): return lax.ppermute(x, axis, pairs)  39.1 us
    ppermute x15, waiting for transfers between devices, shifted(): return lax.ppermute(x, axis, pairs)  11.1 us
    unnamed x31, local copies, waits for them, and re-layouts  10.1 us
    all_gather x1, blocking collectives, prefix(): everything = lax.all_gather(x, axis)  7.22 us
    psum x1, blocking collectives, per_device(): lax.psum((jnp.sum(scaled, axis=1), jnp.sum(scaled * centered, axis=1)), '...  6.62 us
    psum x1, blocking collectives, per_device(): lax.psum((jnp.sum(flat, axis=1), jnp.sum(flat * flat, axis=1)), 'head')  5.66 us
    another operation x1, loops' own time, prefix(): return lax.fori_loop(0, length, step, start)  5.42 us
    dynamic_slice x8, local copies, waits for them, and re-layouts, step(): new = combine(before, everything[k])  4.69 us
  transfers between devices with their start and end apart: 15, of which 4 were waited for; matrix products, arithmetic and copies ran while one was open for 12% of the time, Pallas kernels for 0%

commit v1 on v0

v1 whole, which is shorter than its diff:
```python
import functools

import jax
import jax.numpy as jnp
from jax import lax
from jax.experimental import pallas as pl
from jax.experimental.pallas import tpu as pltpu
from jax.sharding import PartitionSpec as P

norm_eps = 1e-05
f32 = jnp.float32
bf16 = jnp.bfloat16
MESH = pl.DeviceIdType.MESH


def mm(a, b):
    return lax.dot_general(a, b, (((1,), (0,)), ((), ())), preferred_element_type=f32)


def mm_nt(a, b):
    return lax.dot_general(a, b, (((1,), (1,)), ((), ())), preferred_element_type=f32)


def kernel(
    groups,
    head_devices,
    offsets,
    q_in,
    k_in,
    v_in,
    gate_ref,
    cot_ref,
    gaps_ref,
    lists_ref,
    table_ref,
    gain_ref,
    layer_ref,
    dq_ref,
    dk_ref,
    dv_ref,
    dgate_ref,
    qbuf,
    kbuf,
    vbuf,
    gabuf,
    gprev,
    glater,
    sums_out,
    sums_in,
    slope_q,
    slope_k,
    weight_k,
    local_sem,
    gap_send,
    gap_recv,
    q_send,
    q_recv,
    kv_send,
    kv_recv,
    sum_send,
    sum_recv,
    ga_send,
    ga_recv,
):
    rows, feats = q_in.shape
    heads, buckets = table_ref.shape
    head_dim = feats // heads
    scaling = head_dim**-0.5
    full_width = feats * head_devices
    reach = offsets[-1]
    count = len(offsets)
    me = lax.axis_index("seq")
    head = lax.axis_index("head")

    def to_later(d, body):
        pl.when(me + d < groups)(body)

    def to_earlier(d, body):
        pl.when(me >= d)(body)

    barrier = pltpu.get_barrier_semaphore()

    def greet(axis, where):
        pl.semaphore_signal(barrier, inc=1, device_id={axis: where}, device_id_type=MESH)

    for k in range(1, reach + 1):
        to_later(k, lambda k=k: greet("seq", me + k))
        to_earlier(k, lambda k=k: greet("seq", me - k))
    for r in range(1, head_devices):
        greet("head", lax.rem(head + r, head_devices))
    own = [
        pltpu.make_async_copy(src, dst.at[0], local_sem.at[i])
        for i, (src, dst) in enumerate(((q_in, qbuf), (k_in, kbuf), (v_in, vbuf)))
    ]
    for copy in own:
        copy.start()
    pl.semaphore_wait(
        barrier,
        jnp.minimum(me, reach) + jnp.minimum(groups - 1 - me, reach) + head_devices - 1,
    )

    def remote(src, dst, send, recv, axis, where):
        return pltpu.make_async_remote_copy(
            src_ref=src,
            dst_ref=dst,
            send_sem=send,
            recv_sem=recv,
            device_id={axis: where},
            device_id_type=MESH,
        )

    def gaps_up(k):
        return remote(
            gaps_ref, gprev.at[k - 1], gap_send.at[0, k - 1], gap_recv.at[0, k - 1], "seq", me + k
        )

    def gaps_down(k):
        return remote(
            gaps_ref, glater.at[k - 1], gap_send.at[1, k - 1], gap_recv.at[1, k - 1], "seq", me - k
        )

    def keys_up(s):
        return remote(
            k_in, kbuf.at[s + 1], kv_send.at[0, s], kv_recv.at[0, s], "seq", me + offsets[s]
        )

    def values_up(s):
        return remote(
            v_in, vbuf.at[s + 1], kv_send.at[1, s], kv_recv.at[1, s], "seq", me + offsets[s]
        )

    def queries_down(s):
        return remote(q_in, qbuf.at[s + 1], q_send.at[s], q_recv.at[s], "seq", me - offsets[s])

    def grads_down(s):
        return remote(
            gabuf.at[0], gabuf.at[s + 1], ga_send.at[s], ga_recv.at[s], "seq", me - offsets[s]
        )

    def sums_to(r):
        return remote(
            sums_out,
            sums_in.at[r - 1],
            sum_send.at[r - 1],
            sum_recv.at[r - 1],
            "head",
            lax.rem(head + r, head_devices),
        )

    for k in range(1, reach + 1):
        to_later(k, lambda k=k: gaps_up(k).start())
        to_earlier(k, lambda k=k: gaps_down(k).start())
    for s in reversed(range(count)):
        to_later(offsets[s], lambda s=s: keys_up(s).start())
        to_later(offsets[s], lambda s=s: values_up(s).start())
        to_earlier(offsets[s], lambda s=s: queries_down(s).start())

    for k in range(1, reach + 1):

        def no_earlier(k=k):
            gprev[k - 1] = jnp.zeros_like(gprev[k - 1])

        def no_later(k=k):
            glater[k - 1] = jnp.zeros_like(glater[k - 1])

        pl.when(me < k)(no_earlier)
        pl.when(me + k >= groups)(no_later)
    for s, d in enumerate(offsets):

        def no_keys(s=s):
            kbuf[s + 1] = jnp.zeros((rows, feats), bf16)
            vbuf[s + 1] = jnp.zeros((rows, feats), bf16)

        def no_queries(s=s):
            qbuf[s + 1] = jnp.zeros((rows, feats), bf16)
            gabuf[s + 1] = jnp.zeros((feats, rows), bf16)

        pl.when(me < d)(no_keys)
        pl.when(me + d >= groups)(no_queries)

    row_ids = lax.broadcasted_iota(jnp.int32, (rows, rows), 0)
    col_ids = lax.broadcasted_iota(jnp.int32, (rows, rows), 1)
    upper = (row_ids <= col_ids).astype(f32)
    upper_bf = upper.astype(bf16)
    ones = jnp.ones((rows, rows), bf16)
    lane_head = lax.broadcasted_iota(jnp.int32, (rows, feats), 1) // head_dim
    sub_head = lax.broadcasted_iota(jnp.int32, (feats, rows), 0) // head_dim
    lane_masks = [(lane_head == h).astype(bf16) for h in range(heads)]
    sub_masks = [(sub_head == h).astype(bf16) for h in range(heads)]

    def prefix_row(gaps):
        wide = jnp.broadcast_to(gaps, (8, rows)).astype(bf16)
        return mm(wide, upper_bf)[0:1]

    def after_column(gaps):
        return mm(jnp.where(col_ids > row_ids, gaps, 0.0).astype(bf16), ones)

    def bias(delta):
        parts = [jnp.full(delta.shape, table_ref[h, 0], f32) for h in range(heads)]
        for b in range(1, buckets):
            reached = delta >= float(2 ** (b - 1))
            parts = [jnp.where(reached, table_ref[h, b], parts[h]) for h in range(heads)]
        return jnp.concatenate(parts, axis=1)

    def by_head_rows(q):
        return jnp.concatenate([q * mask for mask in lane_masks], axis=0)

    def by_head_lanes(g):
        return jnp.concatenate([g * mask for mask in sub_masks], axis=1)

    def own_heads(wide):
        return jnp.concatenate(
            [
                wide[h * head_dim : (h + 1) * head_dim, h * rows : (h + 1) * rows]
                for h in range(heads)
            ],
            axis=0,
        )

    def activate(keys, queries, biases, mask):
        scores = mm_nt(keys, queries) * scaling + biases
        sig = 0.5 * jnp.tanh(0.5 * scores) + 0.5
        weights = scores * sig
        slope = sig + weights * (1.0 - sig)
        return (weights * mask).astype(bf16), slope * mask

    own_gaps = gaps_ref[...].astype(f32)
    own_total = jnp.sum(own_gaps, axis=1, keepdims=True)
    own_row = prefix_row(own_gaps)
    own_after = after_column(own_gaps)
    diag_bias = bias(own_row + own_after - own_total)
    diag_mask = jnp.concatenate([upper] * heads, axis=1)
    gain = gain_ref[...]
    gates = gate_ref[...].astype(f32)
    upstream = cot_ref[...].astype(f32)
    scaled = (upstream * gates * gain).T

    for copy in own:
        copy.wait()
    keys = kbuf[0]
    values = vbuf[0]
    queries = by_head_rows(qbuf[0])
    diag_weights, diag_slope = activate(keys, queries, diag_bias, diag_mask)
    attended = mm(values.T, diag_weights)

    for k in range(1, reach + 1):
        to_earlier(k, lambda k=k: gaps_up(k).wait_recv())
        to_later(k, lambda k=k: gaps_down(k).wait_recv())

    def between(buf, d):
        if d == 1:
            return jnp.zeros((1, 1), f32)
        return jnp.sum(
            jnp.sum(buf[0 : d - 1].astype(f32), axis=0), axis=1, keepdims=True
        )

    biases = []
    for s, d in enumerate(offsets):
        after = after_column(gprev[d - 1].astype(f32))
        biases.append(bias(own_row + after + between(gprev, d)))
    for s in reversed(range(count)):
        d = offsets[s]
        to_earlier(d, lambda s=s: keys_up(s).wait_recv())
        to_earlier(d, lambda s=s: values_up(s).wait_recv())
    for s in range(count):
        listed = (lists_ref[me, s] >= 0).astype(f32)
        weights, slope = activate(kbuf[s + 1], queries, biases[s], listed)
        slope_q[s] = slope
        attended = attended + mm(vbuf[s + 1].T, weights)

    flat = own_heads(attended)
    own_sums = [
        jnp.sum(x, axis=0, keepdims=True) for x in (flat, flat * flat, scaled, scaled * flat)
    ]
    sums_out[...] = jnp.concatenate(own_sums + [jnp.zeros((4, rows), f32)], axis=0)
    for r in range(1, head_devices):
        sums_to(r).start()

    for s in reversed(range(count)):
        to_later(offsets[s], lambda s=s: queries_down(s).wait_recv())
    for s, d in enumerate(offsets):
        row = prefix_row(glater[d - 1].astype(f32))
        later_bias = bias(row + own_after + between(glater, d))
        there = jnp.minimum(me + d, groups - 1)
        listed = ((lists_ref[there, s] >= 0) & (me + d < groups)).astype(f32)
        weights, slope = activate(keys, by_head_rows(qbuf[s + 1]), later_bias, listed)
        weight_k[s] = weights
        slope_k[s] = slope

    for r in range(1, head_devices):
        sums_to(r).wait_recv()
    sums = sums_out[...]
    for r in range(1, head_devices):
        sums = sums + sums_in[r - 1]
    mean = sums[0:1] / full_width
    var = sums[1:2] / full_width - mean * mean
    inv_std = lax.rsqrt(var + norm_eps)
    centered = (flat - mean) * inv_std
    scaled_mean = sums[2:3] / full_width
    product_mean = inv_std * (sums[3:4] - mean * sums[2:3]) / full_width
    grad = (inv_std * (scaled - scaled_mean - centered * product_mean)).astype(bf16)
    gabuf[0] = grad
    for s in reversed(range(count)):
        to_earlier(offsets[s], lambda s=s: grads_down(s).start())

    grads = by_head_lanes(grad)
    diag_grad = (mm(values, grads) * diag_slope).astype(bf16)
    dq = mm(keys.T, diag_grad)
    dk = mm(diag_grad, queries)
    dv = mm_nt(diag_weights, grads)
    for s in range(count):
        grad_scores = (mm(vbuf[s + 1], grads) * slope_q[s]).astype(bf16)
        dq = dq + mm(kbuf[s + 1].T, grad_scores)
    dq_ref[...] = (own_heads(dq) * scaling).T.astype(bf16)
    normed = centered.T * gain
    layer_ref[...] = (normed * gates).astype(bf16)
    dgate_ref[...] = (upstream * normed).astype(bf16)

    for s in reversed(range(count)):
        to_later(offsets[s], lambda s=s: grads_down(s).wait_recv())
    for s in range(count):
        grads = by_head_lanes(gabuf[s + 1])
        grad_scores = (mm(values, grads) * slope_k[s]).astype(bf16)
        dk = dk + mm(grad_scores, by_head_rows(qbuf[s + 1]))
        dv = dv + mm_nt(weight_k[s], grads)
    dk_ref[...] = (dk * scaling).astype(bf16)
    dv_ref[...] = dv.astype(bf16)

    for k in range(1, reach + 1):
        to_later(k, lambda k=k: gaps_up(k).wait_send())
        to_earlier(k, lambda k=k: gaps_down(k).wait_send())
    for s, d in enumerate(offsets):
        to_later(d, lambda s=s: keys_up(s).wait_send())
        to_later(d, lambda s=s: values_up(s).wait_send())
        to_earlier(d, lambda s=s: queries_down(s).wait_send())
        to_earlier(d, lambda s=s: grads_down(s).wait_send())
    for r in range(1, head_devices):
        sums_to(r).wait_send()


def per_device(
    query_rows,
    key_rows,
    value_rows,
    gate_rows,
    cotangent,
    event_gaps,
    block_lists,
    bias_table,
    norm_gain,
):
    rows, feats = query_rows.shape
    heads = bias_table.shape[0]
    groups = lax.axis_size("seq")
    head_devices = lax.axis_size("head")
    offsets = [2**s for s in range(block_lists.shape[1]) if 2**s < groups]
    count = len(offsets)
    reach = offsets[-1]
    hbm = pl.BlockSpec(memory_space=pl.ANY)
    vmem = pl.BlockSpec(memory_space=pltpu.VMEM)
    smem = pl.BlockSpec(memory_space=pltpu.SMEM)
    dma = pltpu.SemaphoreType.DMA
    return pl.pallas_call(
        functools.partial(kernel, groups, head_devices, offsets),
        out_shape=[jax.ShapeDtypeStruct((rows, feats), bf16)] * 5,
        in_specs=[hbm, hbm, hbm, vmem, vmem, vmem, smem, smem, vmem],
        out_specs=[vmem] * 5,
        scratch_shapes=[
            pltpu.VMEM((count + 1, rows, feats), bf16),
            pltpu.VMEM((count + 1, rows, feats), bf16),
            pltpu.VMEM((count + 1, rows, feats), bf16),
            pltpu.VMEM((count + 1, feats, rows), bf16),
            pltpu.VMEM((reach, 1, rows), jnp.int32),
            pltpu.VMEM((reach, 1, rows), jnp.int32),
            pltpu.VMEM((8, rows), f32),
            pltpu.VMEM((head_devices - 1, 8, rows), f32),
            pltpu.VMEM((count, rows, heads * rows), f32),
            pltpu.VMEM((count, rows, heads * rows), f32),
            pltpu.VMEM((count, rows, heads * rows), bf16),
            dma((3,)),
            dma((2, reach)),
            dma((2, reach)),
            dma((count,)),
            dma((count,)),
            dma((2, count)),
            dma((2, count)),
            dma((head_devices - 1,)),
            dma((head_devices - 1,)),
            dma((count,)),
            dma((count,)),
        ],
        compiler_params=pltpu.CompilerParams(
            collective_id=0, has_side_effects=True, vmem_limit_bytes=24 * 2**20
        ),
    )(
        query_rows,
        key_rows,
        value_rows,
        gate_rows,
        cotangent,
        event_gaps.reshape(1, rows),
        block_lists,
        bias_table,
        norm_gain.reshape(1, feats),
    )


def solution(mesh):
    placed = P("seq", "head")
    return jax.shard_map(
        per_device,
        mesh=mesh,
        in_specs=(
            placed,
            placed,
            placed,
            placed,
            placed,
            P("seq"),
            P(),
            P("head", None),
            P("head"),
        ),
        out_specs=(placed,) * 5,
        check_vma=False,
    )
```

time: 97.1 us -> 30.8 us (0.32)
  starting transfers between devices: 39.1 us -> 0 us
  Pallas kernels: 0 us -> 21.4 us
  blocking collectives: 19.5 us -> 0 us
  waiting for transfers between devices: 11.1 us -> 0 us
  local copies, waits for them, and re-layouts: 16.5 us -> 8.22 us
  loops' own time: 5.53 us -> 0 us
  between operations: 3.04 us -> 0.68 us
  matrix products: 1.12 us -> 0 us
    ppermute x15 -> x0, starting transfers between devices: 39.1 us -> none  [shifted(): return lax.ppermute(x, axis, pairs)]
    pallas_call x0 -> x1, Pallas kernels: none -> 21.4 us  [per_device(): pl.pallas_call(functools.partial(kernel, groups, head_devices, offsets),...]
    psum x2 -> x0, blocking collectives: 12.3 us -> none  [the longest x1 6.62 us: per_device(): lax.psum((jnp.sum(scaled, axis=1), jnp.sum(scaled * centered, axis=1)), '...]
    ppermute x15 -> x0, waiting for transfers between devices: 11.1 us -> none  [shifted(): return lax.ppermute(x, axis, pairs)]
    all_gather x1 -> x0, blocking collectives: 7.22 us -> none  [prefix(): everything = lax.all_gather(x, axis)]
    another operation x7 -> x0, loops' own time: 5.53 us -> none  [the longest x1 5.42 us: prefix(): return lax.fori_loop(0, length, step, start)]
    dynamic_slice x9 -> x0, local copies, waits for them, and re-layouts: 4.71 us -> none  [the longest x8 4.69 us: step(): new = combine(before, everything[k])]
    unnamed x31 -> x23, local copies, waits for them, and re-layouts: 10.1 us -> 8.22 us
  transfers between devices with their start and end apart: 15 -> 0, of which waited for: 4 -> 0; matrix products, arithmetic and copies ran while one was open for 12% -> 0% of each run, Pallas kernels for 0% -> 0%
where the time goes in v1:
time: 30.8 us; the launch traced here: 30.3 us
  Pallas kernels  21.4 us (69%)
  local copies, waits for them, and re-layouts  8.22 us (27%)
  between operations  0.68 us (2%)
    pallas_call x1, Pallas kernels, per_device(): pl.pallas_call(functools.partial(kernel, groups, head_devices, offsets),...  21.4 us
    unnamed x23, local copies, waits for them, and re-layouts  8.22 us

profile of v1, /device:TPU:0, one launch (start us, length us, event | category | flops | bytes accessed | tf_op | source)
XLA Modules:
  0.0 30.3 jit_solution(14347109029769480043)
XLA Ops:
  0.6 0.0 copy-start.8
  0.6 0.0 copy-start.6
  0.7 0.0 copy-start.7
  0.7 0.6 %copy-done.8 = f32[128]{0:T(128)S(1)} copy-done((f32[128]{0:T(128)S(1)}, f32[128]{0:T(128)}, u32[]{:S(2)}) %copy-start.8) | copy-done | bytes 536
  1.3 0.0 copy-done.6
  1.3 0.0 copy-done.7
  1.3 0.0 copy-start
  1.3 0.8 %copy-done = bf16[128,128]{1,0:T(8,128)(2,1)S(1)} copy-done((bf16[128,128]{1,0:T(8,128)(2,1)S(1)}, bf16[128,128]{1,0:T(8,128)(2,1)}, u32[]{:S(2)}) %copy-start) | copy-done | bytes 32792
  2.1 0.0 copy-start.1
  2.1 0.8 %copy-done.1 = bf16[128,128]{1,0:T(8,128)(2,1)S(1)} copy-done((bf16[128,128]{1,0:T(8,128)(2,1)S(1)}, bf16[128,128]{1,0:T(8,128)(2,1)}, u32[]{:S(2)}) %copy-start.1) | copy-done | bytes 32792
  2.9 0.0 copy-start.2
  2.9 0.8 %copy-done.2 = bf16[128,128]{1,0:T(8,128)(2,1)S(1)} copy-done((bf16[128,128]{1,0:T(8,128)(2,1)S(1)}, bf16[128,128]{1,0:T(8,128)(2,1)}, u32[]{:S(2)}) %copy-start.2) | copy-done | bytes 32792
  3.6 0.0 copy-start.3
  3.6 0.8 %copy-done.3 = bf16[128,128]{1,0:T(8,128)(2,1)S(1)} copy-done((bf16[128,128]{1,0:T(8,128)(2,1)S(1)}, bf16[128,128]{1,0:T(8,128)(2,1)}, u32[]{:S(2)}) %copy-start.3) | copy-done | bytes 32792
  4.4 0.0 copy-start.4
  4.4 0.8 %copy-done.4 = bf16[128,128]{1,0:T(8,128)(2,1)S(1)} copy-done((bf16[128,128]{1,0:T(8,128)(2,1)S(1)}, bf16[128,128]{1,0:T(8,128)(2,1)}, u32[]{:S(2)}) %copy-start.4) | copy-done | bytes 32792
  5.1 0.0 copy-start.5
  5.1 0.7 %copy-done.5 = s32[8,8]{1,0:T(8,128)S(1)} copy-done((s32[8,8]{1,0:T(8,128)S(1)}, s32[8,8]{1,0:T(8,128)}, u32[]{:S(2)}) %copy-start.5) | copy-done | bytes 280
  5.8 21.4 %shard_map.128 = (bf16[128,128]{1,0:T(8,128)(2,1)S(1)}, bf16[128,128]{1,0:T(8,128)(2,1)S(1)}, bf16[128,128]{1,0:T(8,128)(2,1)S(1)}, bf16[128,128]{1,0:T(8,128)(2,1)S(1)}, bf16[128,128]{1,0:T(8,128)(2,1)S(1)}) custom-call(bf16[128,128]{1,0:T(8,128)(2,1)S(1)} %copy-done, bf16[128,128]{1,0:T(8,128)(2,1)S(1)} %copy-done.1, bf16[128,128]{1,0:T(8,128)(2,1)S(1)} %copy-done.2, ...), custom_call_target="tpu_custom_call" | custom-call | tf_op jit(solution)/shard_map/pallas_call | solution.py:363
  27.2 0.6 %copy.19 = bf16[128,128]{1,0:T(8,128)(2,1)} copy(bf16[128,128]{1,0:T(8,128)(2,1)S(1)} %get-tuple-element.10) | data formatting | bytes 65536
  27.9 0.6 %copy.20 = bf16[128,128]{1,0:T(8,128)(2,1)} copy(bf16[128,128]{1,0:T(8,128)(2,1)S(1)} %get-tuple-element.11) | data formatting | bytes 65536
  28.5 0.6 %copy.21 = bf16[128,128]{1,0:T(8,128)(2,1)} copy(bf16[128,128]{1,0:T(8,128)(2,1)S(1)} %get-tuple-element.12) | data formatting | bytes 65536
  29.1 0.6 %copy.22 = bf16[128,128]{1,0:T(8,128)(2,1)} copy(bf16[128,128]{1,0:T(8,128)(2,1)S(1)} %get-tuple-element.13) | data formatting | bytes 65536
  29.7 0.6 %copy.23 = bf16[128,128]{1,0:T(8,128)(2,1)} copy(bf16[128,128]{1,0:T(8,128)(2,1)S(1)} %get-tuple-element.14) | data formatting | bytes 65536
Async XLA Ops:
  0.6 0.7 %copy-start.8 = (f32[128]{0:T(128)S(1)}, f32[128]{0:T(128)}, u32[]{:S(2)}) copy-start(f32[128]{0:T(128)} %param.17) | copy-start | bytes 1540
  0.6 0.7 %copy-start.6 = (f32[2,16]{1,0:T(2,128)S(1)}, f32[2,16]{1,0:T(2,128)}, u32[]{:S(2)}) copy-start(f32[2,16]{1,0:T(2,128)} %table_ref.1) | copy-start | bytes 388
  0.7 0.7 %copy-start.7 = (s32[128]{0:T(128)S(1)}, s32[128]{0:T(128)}, u32[]{:S(2)}) copy-start(s32[128]{0:T(128)} %param.14) | copy-start | bytes 1540
  1.3 0.8 %copy-start = (bf16[128,128]{1,0:T(8,128)(2,1)S(1)}, bf16[128,128]{1,0:T(8,128)(2,1)}, u32[]{:S(2)}) copy-start(bf16[128,128]{1,0:T(8,128)(2,1)} %q_in.1) | copy-start | bytes 98308
  2.1 0.8 %copy-start.1 = (bf16[128,128]{1,0:T(8,128)(2,1)S(1)}, bf16[128,128]{1,0:T(8,128)(2,1)}, u32[]{:S(2)}) copy-start(bf16[128,128]{1,0:T(8,128)(2,1)} %k_in.1) | copy-start | bytes 98308
  2.9 0.8 %copy-start.2 = (bf16[128,128]{1,0:T(8,128)(2,1)S(1)}, bf16[128,128]{1,0:T(8,128)(2,1)}, u32[]{:S(2)}) copy-start(bf16[128,128]{1,0:T(8,128)(2,1)} %v_in.1) | copy-start | bytes 98308
  3.6 0.8 %copy-start.3 = (bf16[128,128]{1,0:T(8,128)(2,1)S(1)}, bf16[128,128]{1,0:T(8,128)(2,1)}, u32[]{:S(2)}) copy-start(bf16[128,128]{1,0:T(8,128)(2,1)} %gate_ref.1) | copy-start | bytes 98308
  4.4 0.8 %copy-start.4 = (bf16[128,128]{1,0:T(8,128)(2,1)S(1)}, bf16[128,128]{1,0:T(8,128)(2,1)}, u32[]{:S(2)}) copy-start(bf16[128,128]{1,0:T(8,128)(2,1)} %cot_ref.1) | copy-start | bytes 98308
  5.1 0.7 %copy-start.5 = (s32[8,8]{1,0:T(8,128)S(1)}, s32[8,8]{1,0:T(8,128)}, u32[]{:S(2)}) copy-start(s32[8,8]{1,0:T(8,128)} %lists_ref.1) | copy-start | bytes 772

commit v2 on v1

--- a/solution.py
+++ b/solution.py
@@ -28,17 +28,23 @@
     q_in,
     k_in,
     v_in,
-    gate_ref,
-    cot_ref,
-    gaps_ref,
-    lists_ref,
-    table_ref,
-    gain_ref,
+    gate_in,
+    cot_in,
+    gaps_in,
+    lists_in,
+    table_in,
+    gain_in,
     layer_ref,
     dq_ref,
     dk_ref,
     dv_ref,
     dgate_ref,
+    gate_ref,
+    cot_ref,
+    gaps_ref,
+    gain_ref,
+    lists_ref,
+    table_ref,
     qbuf,
     kbuf,
     vbuf,
@@ -50,6 +56,10 @@
     slope_q,
     slope_k,
     weight_k,
+    att_acc,
+    dq_acc,
+    dk_acc,
+    dv_acc,
     local_sem,
     gap_send,
     gap_recv,
@@ -63,7 +73,7 @@
     ga_recv,
 ):
     rows, feats = q_in.shape
-    heads, buckets = table_ref.shape
+    heads, buckets = table_in.shape
     head_dim = feats // heads
     scaling = head_dim**-0.5
     full_width = feats * head_devices
@@ -78,6 +88,21 @@
     def to_earlier(d, body):
         pl.when(me >= d)(body)
 
+    pairs = (
+        (gaps_in, gaps_ref),
+        (table_in, table_ref),
+        (lists_in, lists_ref),
+        (gain_in, gain_ref),
+        (k_in, kbuf.at[0]),
+        (q_in, qbuf.at[0]),
+        (v_in, vbuf.at[0]),
+        (gate_in, gate_ref),
+        (cot_in, cot_ref),
+    )
+    own = [pltpu.make_async_copy(src, dst, local_sem.at[i]) for i, (src, dst) in enumerate(pairs)]
+    for copy in own:
+        copy.start()
+
     barrier = pltpu.get_barrier_semaphore()
 
     def greet(axis, where):
@@ -88,12 +113,6 @@
         to_earlier(k, lambda k=k: greet("seq", me - k))
     for r in range(1, head_devices):
         greet("head", lax.rem(head + r, head_devices))
-    own = [
-        pltpu.make_async_copy(src, dst.at[0], local_sem.at[i])
-        for i, (src, dst) in enumerate(((q_in, qbuf), (k_in, kbuf), (v_in, vbuf)))
-    ]
-    for copy in own:
-        copy.start()
     pl.semaphore_wait(
         barrier,
         jnp.minimum(me, reach) + jnp.minimum(groups - 1 - me, reach) + head_devices - 1,
@@ -111,12 +130,12 @@
 
     def gaps_up(k):
         return remote(
-            gaps_ref, gprev.at[k - 1], gap_send.at[0, k - 1], gap_recv.at[0, k - 1], "seq", me + k
+            gaps_in, gprev.at[k - 1], gap_send.at[0, k - 1], gap_recv.at[0, k - 1], "seq", me + k
         )
 
     def gaps_down(k):
         return remote(
-            gaps_ref, glater.at[k - 1], gap_send.at[1, k - 1], gap_recv.at[1, k - 1], "seq", me - k
+            gaps_in, glater.at[k - 1], gap_send.at[1, k - 1], gap_recv.at[1, k - 1], "seq", me - k
         )
 
     def keys_up(s):
@@ -150,7 +169,7 @@
     for k in range(1, reach + 1):
         to_later(k, lambda k=k: gaps_up(k).start())
         to_earlier(k, lambda k=k: gaps_down(k).start())
-    for s in reversed(range(count)):
+    for s in range(count):
         to_later(offsets[s], lambda s=s: keys_up(s).start())
         to_later(offsets[s], lambda s=s: values_up(s).start())
         to_earlier(offsets[s], lambda s=s: queries_down(s).start())
@@ -165,18 +184,6 @@
 
         pl.when(me < k)(no_earlier)
         pl.when(me + k >= groups)(no_later)
-    for s, d in enumerate(offsets):
-
-        def no_keys(s=s):
-            kbuf[s + 1] = jnp.zeros((rows, feats), bf16)
-            vbuf[s + 1] = jnp.zeros((rows, feats), bf16)
-
-        def no_queries(s=s):
-            qbuf[s + 1] = jnp.zeros((rows, feats), bf16)
-            gabuf[s + 1] = jnp.zeros((feats, rows), bf16)
-
-        pl.when(me < d)(no_keys)
-        pl.when(me + d >= groups)(no_queries)
 
     row_ids = lax.broadcasted_iota(jnp.int32, (rows, rows), 0)
     col_ids = lax.broadcasted_iota(jnp.int32, (rows, rows), 1)
@@ -224,6 +231,8 @@
         slope = sig + weights * (1.0 - sig)
         return (weights * mask).astype(bf16), slope * mask
 
+    for copy in own:
+        copy.wait()
     own_gaps = gaps_ref[...].astype(f32)
     own_total = jnp.sum(own_gaps, axis=1, keepdims=True)
     own_row = prefix_row(own_gaps)
@@ -235,13 +244,11 @@
     upstream = cot_ref[...].astype(f32)
     scaled = (upstream * gates * gain).T
 
-    for copy in own:
-        copy.wait()
     keys = kbuf[0]
     values = vbuf[0]
     queries = by_head_rows(qbuf[0])
     diag_weights, diag_slope = activate(keys, queries, diag_bias, diag_mask)
-    attended = mm(values.T, diag_weights)
+    att_acc[...] = mm(values.T, diag_weights)
 
     for k in range(1, reach + 1):
         to_earlier(k, lambda k=k: gaps_up(k).wait_recv())
@@ -258,17 +265,19 @@
     for s, d in enumerate(offsets):
         after = after_column(gprev[d - 1].astype(f32))
         biases.append(bias(own_row + after + between(gprev, d)))
-    for s in reversed(range(count)):
-        d = offsets[s]
-        to_earlier(d, lambda s=s: keys_up(s).wait_recv())
-        to_earlier(d, lambda s=s: values_up(s).wait_recv())
-    for s in range(count):
-        listed = (lists_ref[me, s] >= 0).astype(f32)
-        weights, slope = activate(kbuf[s + 1], queries, biases[s], listed)
-        slope_q[s] = slope
-        attended = attended + mm(vbuf[s + 1].T, weights)
-
-    flat = own_heads(attended)
+    for s, d in enumerate(offsets):
+
+        def attend(s=s):
+            keys_up(s).wait_recv()
+            listed = (lists_ref[me, s] >= 0).astype(f32)
+            weights, slope = activate(kbuf[s + 1], queries, biases[s], listed)
+            slope_q[s] = slope
+            values_up(s).wait_recv()
+            att_acc[...] += mm(vbuf[s + 1].T, weights)
+
+        to_earlier(d, attend)
+
+    flat = own_heads(att_acc[...])
     own_sums = [
         jnp.sum(x, axis=0, keepdims=True) for x in (flat, flat * flat, scaled, scaled * flat)
     ]
@@ -276,16 +285,18 @@
     for r in range(1, head_devices):
         sums_to(r).start()
 
-    for s in reversed(range(count)):
-        to_later(offsets[s], lambda s=s: queries_down(s).wait_recv())
-    for s, d in enumerate(offsets):
-        row = prefix_row(glater[d - 1].astype(f32))
-        later_bias = bias(row + own_after + between(glater, d))
-        there = jnp.minimum(me + d, groups - 1)
-        listed = ((lists_ref[there, s] >= 0) & (me + d < groups)).astype(f32)
-        weights, slope = activate(keys, by_head_rows(qbuf[s + 1]), later_bias, listed)
-        weight_k[s] = weights
-        slope_k[s] = slope
+    for s, d in enumerate(offsets):
+
+        def score_later(s=s, d=d):
+            row = prefix_row(glater[d - 1].astype(f32))
+            later_bias = bias(row + own_after + between(glater, d))
+            listed = (lists_ref[me + d, s] >= 0).astype(f32)
+            queries_down(s).wait_recv()
+            weights, slope = activate(keys, by_head_rows(qbuf[s + 1]), later_bias, listed)
+            weight_k[s] = weights
+            slope_k[s] = slope
+
+        to_later(d, score_later)
 
     for r in range(1, head_devices):
         sums_to(r).wait_recv()
@@ -300,31 +311,38 @@
     product_mean = inv_std * (sums[3:4] - mean * sums[2:3]) / full_width
     grad = (inv_std * (scaled - scaled_mean - centered * product_mean)).astype(bf16)
     gabuf[0] = grad
-    for s in reversed(range(count)):
+    for s in range(count):
         to_earlier(offsets[s], lambda s=s: grads_down(s).start())
 
     grads = by_head_lanes(grad)
     diag_grad = (mm(values, grads) * diag_slope).astype(bf16)
-    dq = mm(keys.T, diag_grad)
-    dk = mm(diag_grad, queries)
-    dv = mm_nt(diag_weights, grads)
-    for s in range(count):
-        grad_scores = (mm(vbuf[s + 1], grads) * slope_q[s]).astype(bf16)
-        dq = dq + mm(kbuf[s + 1].T, grad_scores)
-    dq_ref[...] = (own_heads(dq) * scaling).T.astype(bf16)
+    dq_acc[...] = mm(keys.T, diag_grad)
+    dk_acc[...] = mm(diag_grad, queries)
+    dv_acc[...] = mm_nt(diag_weights, grads)
+    for s, d in enumerate(offsets):
+
+        def query_part(s=s):
+            grad_scores = (mm(vbuf[s + 1], grads) * slope_q[s]).astype(bf16)
+            dq_acc[...] += mm(kbuf[s + 1].T, grad_scores)
+
+        to_earlier(d, query_part)
+    dq_ref[...] = (own_heads(dq_acc[...]) * scaling).T.astype(bf16)
     normed = centered.T * gain
     layer_ref[...] = (normed * gates).astype(bf16)
     dgate_ref[...] = (upstream * normed).astype(bf16)
 
-    for s in reversed(range(count)):
-        to_later(offsets[s], lambda s=s: grads_down(s).wait_recv())
-    for s in range(count):
-        grads = by_head_lanes(gabuf[s + 1])
-        grad_scores = (mm(values, grads) * slope_k[s]).astype(bf16)
-        dk = dk + mm(grad_scores, by_head_rows(qbuf[s + 1]))
-        dv = dv + mm_nt(weight_k[s], grads)
-    dk_ref[...] = (dk * scaling).astype(bf16)
-    dv_ref[...] = dv.astype(bf16)
+    for s, d in enumerate(offsets):
+
+        def key_part(s=s):
+            grads_down(s).wait_recv()
+            grads = by_head_lanes(gabuf[s + 1])
+            grad_scores = (mm(values, grads) * slope_k[s]).astype(bf16)
+            dk_acc[...] += mm(grad_scores, by_head_rows(qbuf[s + 1]))
+            dv_acc[...] += mm_nt(weight_k[s], grads)
+
+        to_later(d, key_part)
+    dk_ref[...] = (dk_acc[...] * scaling).astype(bf16)
+    dv_ref[...] = dv_acc[...].astype(bf16)
 
     for k in range(1, reach + 1):
         to_later(k, lambda k=k: gaps_up(k).wait_send())
@@ -336,6 +354,15 @@
         to_earlier(d, lambda s=s: grads_down(s).wait_send())
     for r in range(1, head_devices):
         sums_to(r).wait_send()
+
+
+def hand_out(*refs):
+    sems = refs[-1]
+    copies = [pltpu.make_async_copy(refs[i], refs[i + 5], sems.at[i]) for i in range(5)]
+    for copy in copies:
+        copy.start()
+    for copy in copies:
+        copy.wait()
 
 
 def per_device(
@@ -356,16 +383,32 @@
     offsets = [2**s for s in range(block_lists.shape[1]) if 2**s < groups]
     count = len(offsets)
     reach = offsets[-1]
-    hbm = pl.BlockSpec(memory_space=pl.ANY)
+    hbm = pl.BlockSpec(memory_space=pltpu.HBM)
     vmem = pl.BlockSpec(memory_space=pltpu.VMEM)
-    smem = pl.BlockSpec(memory_space=pltpu.SMEM)
     dma = pltpu.SemaphoreType.DMA
-    return pl.pallas_call(
+    operands = (
+        query_rows,
+        key_rows,
+        value_rows,
+        gate_rows,
+        cotangent,
+        event_gaps.reshape(1, rows),
+        block_lists,
+        bias_table,
+        norm_gain.reshape(1, feats),
+    )
+    results = pl.pallas_call(
         functools.partial(kernel, groups, head_devices, offsets),
-        out_shape=[jax.ShapeDtypeStruct((rows, feats), bf16)] * 5,
-        in_specs=[hbm, hbm, hbm, vmem, vmem, vmem, smem, smem, vmem],
+        out_shape=[pltpu.VMEM((rows, feats), bf16)] * 5,
+        in_specs=[hbm] * 9,
         out_specs=[vmem] * 5,
         scratch_shapes=[
+            pltpu.VMEM((rows, feats), bf16),
+            pltpu.VMEM((rows, feats), bf16),
+            pltpu.VMEM((1, rows), jnp.int32),
+            pltpu.VMEM((1, feats), f32),
+            pltpu.SMEM(block_lists.shape, jnp.int32),
+            pltpu.SMEM(bias_table.shape, f32),
             pltpu.VMEM((count + 1, rows, feats), bf16),
             pltpu.VMEM((count + 1, rows, feats), bf16),
             pltpu.VMEM((count + 1, rows, feats), bf16),
@@ -377,7 +420,11 @@
             pltpu.VMEM((count, rows, heads * rows), f32),
             pltpu.VMEM((count, rows, heads * rows), f32),
             pltpu.VMEM((count, rows, heads * rows), bf16),
-            dma((3,)),
+            pltpu.VMEM((feats, heads * rows), f32),
+            pltpu.VMEM((feats, heads * rows), f32),
+            pltpu.VMEM((rows, feats), f32),
+            pltpu.VMEM((rows, feats), f32),
+            dma((9,)),
             dma((2, reach)),
             dma((2, reach)),
             dma((count,)),
@@ -392,17 +439,14 @@
         compiler_params=pltpu.CompilerParams(
             collective_id=0, has_side_effects=True, vmem_limit_bytes=24 * 2**20
         ),
-    )(
-        query_rows,
-        key_rows,
-        value_rows,
-        gate_rows,
-        cotangent,
-        event_gaps.reshape(1, rows),
-        block_lists,
-        bias_table,
-        norm_gain.reshape(1, feats),
-    )
+    )(*[pltpu.with_memory_space_constraint(x, pltpu.HBM) for x in operands])
+    return pl.pallas_call(
+        hand_out,
+        out_shape=[jax.ShapeDtypeStruct((rows, feats), bf16)] * 5,
+        in_specs=[vmem] * 5,
+        out_specs=[hbm] * 5,
+        scratch_shapes=[dma((5,))],
+    )(*results)
 
 
 def solution(mesh):

time: 30.8 us -> 26.4 us (0.86)
  local copies, waits for them, and re-layouts: 8.22 us -> 3.01 us
  Pallas kernels: 21.4 us -> 22.5 us
    unnamed x23 -> x10, local copies, waits for them, and re-layouts: 8.22 us -> 3.01 us
    pallas_call x0 -> x1, Pallas kernels: none -> 1.52 us  [per_device(): pl.pallas_call(hand_out, out_shape=[jax.ShapeDtypeStruct((rows, feats), b...]
    pallas_call x1, Pallas kernels: 21.4 us -> 21 us  [per_device(): pl.pallas_call(functools.partial(kernel, groups, head_devices, offsets),...]
where the time goes in v2:
time: 26.4 us; the launch traced here: 26.2 us
  Pallas kernels  22.5 us (85%)
  local copies, waits for them, and re-layouts  3.01 us (11%)
  between operations  0.66 us (2%)
    pallas_call x1, Pallas kernels, per_device(): pl.pallas_call(functools.partial(kernel, groups, head_devices, offsets),...  21 us
    unnamed x10, local copies, waits for them, and re-layouts  3.01 us
    pallas_call x1, Pallas kernels, per_device(): pl.pallas_call(hand_out, out_shape=[jax.ShapeDtypeStruct((rows, feats), b...  1.52 us

profile of v2, /device:TPU:0, one launch (start us, length us, event | category | flops | bytes accessed | tf_op | source)
XLA Modules:
  0.0 26.2 jit_solution(44792436423516383)
XLA Ops:
  0.6 21.0 %shard_map.128 = (bf16[128,128]{1,0:T(8,128)(2,1)S(1)}, bf16[128,128]{1,0:T(8,128)(2,1)S(1)}, bf16[128,128]{1,0:T(8,128)(2,1)S(1)}, bf16[128,128]{1,0:T(8,128)(2,1)S(1)}, bf16[128,128]{1,0:T(8,128)(2,1)S(1)}) custom-call(bf16[128,128]{1,0:T(8,128)(2,1)} %q_in.1, bf16[128,128]{1,0:T(8,128)(2,1)} %k_in.1, bf16[128,128]{1,0:T(8,128)(2,1)} %v_in.1, ...), custom_call_target="tpu_custom_call" | custom-call | tf_op jit(solution)/shard_map/pallas_call | solution.py:400
  21.7 0.0 copy-start
  21.7 0.6 %copy-done = bf16[128,128]{1,0:T(8,128)(2,1)} copy-done((bf16[128,128]{1,0:T(8,128)(2,1)}, bf16[128,128]{1,0:T(8,128)(2,1)S(1)}, u32[]{:S(2)}) %copy-start) | copy-done | bytes 32792
  22.3 0.0 copy-start.1
  22.3 0.6 %copy-done.1 = bf16[128,128]{1,0:T(8,128)(2,1)} copy-done((bf16[128,128]{1,0:T(8,128)(2,1)}, bf16[128,128]{1,0:T(8,128)(2,1)S(1)}, u32[]{:S(2)}) %copy-start.1) | copy-done | bytes 32792
  22.9 0.0 copy-start.2
  22.9 0.6 %copy-done.2 = bf16[128,128]{1,0:T(8,128)(2,1)} copy-done((bf16[128,128]{1,0:T(8,128)(2,1)}, bf16[128,128]{1,0:T(8,128)(2,1)S(1)}, u32[]{:S(2)}) %copy-start.2) | copy-done | bytes 32792
  23.5 0.0 copy-start.3
  23.5 0.6 %copy-done.3 = bf16[128,128]{1,0:T(8,128)(2,1)} copy-done((bf16[128,128]{1,0:T(8,128)(2,1)}, bf16[128,128]{1,0:T(8,128)(2,1)S(1)}, u32[]{:S(2)}) %copy-start.3) | copy-done | bytes 32792
  24.1 0.0 copy-start.4
  24.1 0.6 %copy-done.4 = bf16[128,128]{1,0:T(8,128)(2,1)} copy-done((bf16[128,128]{1,0:T(8,128)(2,1)}, bf16[128,128]{1,0:T(8,128)(2,1)S(1)}, u32[]{:S(2)}) %copy-start.4) | copy-done | bytes 32792
  24.7 1.5 %shard_map.129 = (bf16[128,128]{1,0:T(8,128)(2,1)}, bf16[128,128]{1,0:T(8,128)(2,1)}, bf16[128,128]{1,0:T(8,128)(2,1)}, bf16[128,128]{1,0:T(8,128)(2,1)}, bf16[128,128]{1,0:T(8,128)(2,1)}) custom-call(bf16[128,128]{1,0:T(8,128)(2,1)} %copy-done, bf16[128,128]{1,0:T(8,128)(2,1)} %copy-done.1, bf16[128,128]{1,0:T(8,128)(2,1)} %copy-done.2, ...), custom_call_target="tpu_custom_call" | custom-call | tf_op jit(solution)/shard_map/pallas_call | solution.py:443
Async XLA Ops:
  21.7 0.6 %copy-start = (bf16[128,128]{1,0:T(8,128)(2,1)}, bf16[128,128]{1,0:T(8,128)(2,1)S(1)}, u32[]{:S(2)}) copy-start(bf16[128,128]{1,0:T(8,128)(2,1)S(1)} %get-tuple-element.10.refs_0_) | copy-start | bytes 98308
  22.3 0.6 %copy-start.1 = (bf16[128,128]{1,0:T(8,128)(2,1)}, bf16[128,128]{1,0:T(8,128)(2,1)S(1)}, u32[]{:S(2)}) copy-start(bf16[128,128]{1,0:T(8,128)(2,1)S(1)} %get-tuple-element.11.refs_1_) | copy-start | bytes 98308
  22.9 0.6 %copy-start.2 = (bf16[128,128]{1,0:T(8,128)(2,1)}, bf16[128,128]{1,0:T(8,128)(2,1)S(1)}, u32[]{:S(2)}) copy-start(bf16[128,128]{1,0:T(8,128)(2,1)S(1)} %get-tuple-element.12.refs_2_) | copy-start | bytes 98308
  23.5 0.6 %copy-start.3 = (bf16[128,128]{1,0:T(8,128)(2,1)}, bf16[128,128]{1,0:T(8,128)(2,1)S(1)}, u32[]{:S(2)}) copy-start(bf16[128,128]{1,0:T(8,128)(2,1)S(1)} %get-tuple-element.13.refs_3_) | copy-start | bytes 98308
  24.1 0.6 %copy-start.4 = (bf16[128,128]{1,0:T(8,128)(2,1)}, bf16[128,128]{1,0:T(8,128)(2,1)S(1)}, u32[]{:S(2)}) copy-start(bf16[128,128]{1,0:T(8,128)(2,1)S(1)} %get-tuple-element.14.refs_4_) | copy-start | bytes 98308

commit v3 on v2

--- a/solution.py
+++ b/solution.py
@@ -267,26 +267,6 @@
         biases.append(bias(own_row + after + between(gprev, d)))
     for s, d in enumerate(offsets):
 
-        def attend(s=s):
-            keys_up(s).wait_recv()
-            listed = (lists_ref[me, s] >= 0).astype(f32)
-            weights, slope = activate(kbuf[s + 1], queries, biases[s], listed)
-            slope_q[s] = slope
-            values_up(s).wait_recv()
-            att_acc[...] += mm(vbuf[s + 1].T, weights)
-
-        to_earlier(d, attend)
-
-    flat = own_heads(att_acc[...])
-    own_sums = [
-        jnp.sum(x, axis=0, keepdims=True) for x in (flat, flat * flat, scaled, scaled * flat)
-    ]
-    sums_out[...] = jnp.concatenate(own_sums + [jnp.zeros((4, rows), f32)], axis=0)
-    for r in range(1, head_devices):
-        sums_to(r).start()
-
-    for s, d in enumerate(offsets):
-
         def score_later(s=s, d=d):
             row = prefix_row(glater[d - 1].astype(f32))
             later_bias = bias(row + own_after + between(glater, d))
@@ -297,6 +277,26 @@
             slope_k[s] = slope
 
         to_later(d, score_later)
+
+    for s, d in enumerate(offsets):
+
+        def attend(s=s):
+            keys_up(s).wait_recv()
+            listed = (lists_ref[me, s] >= 0).astype(f32)
+            weights, slope = activate(kbuf[s + 1], queries, biases[s], listed)
+            slope_q[s] = slope
+            values_up(s).wait_recv()
+            att_acc[...] += mm(vbuf[s + 1].T, weights)
+
+        to_earlier(d, attend)
+
+    flat = own_heads(att_acc[...])
+    own_sums = [
+        jnp.sum(x, axis=0, keepdims=True) for x in (flat, flat * flat, scaled, scaled * flat)
+    ]
+    sums_out[...] = jnp.concatenate(own_sums + [jnp.zeros((4, rows), f32)], axis=0)
+    for r in range(1, head_devices):
+        sums_to(r).start()
 
     for r in range(1, head_devices):
         sums_to(r).wait_recv()
@@ -446,7 +446,8 @@
         in_specs=[vmem] * 5,
         out_specs=[hbm] * 5,
         scratch_shapes=[dma((5,))],
-    )(*results)
+        compiler_params=pltpu.CompilerParams(vmem_limit_bytes=2**20),
+    )(*[pltpu.with_memory_space_constraint(x, pltpu.VMEM) for x in results])
 
 
 def solution(mesh):

time: 26.4 us -> 22.5 us (0.85)
  local copies, waits for them, and re-layouts: 3.01 us -> 0 us
  Pallas kernels: 22.5 us -> 21.7 us
    unnamed x10 -> x0, local copies, waits for them, and re-layouts: 3.01 us -> none
    pallas_call x1, Pallas kernels: 1.52 us -> 0.71 us  [per_device(): pl.pallas_call(hand_out, out_shape=[jax.ShapeDtypeStruct((rows, feats), b...]
where the time goes in v3:
time: 22.5 us; the launch traced here: 22.4 us
  Pallas kernels  21.7 us (96%)
  between operations  0.64 us (3%)
    pallas_call x1, Pallas kernels, per_device(): pl.pallas_call(functools.partial(kernel, groups, head_devices, offsets),...  21 us
    pallas_call x1, Pallas kernels, per_device(): pl.pallas_call(hand_out, out_shape=[jax.ShapeDtypeStruct((rows, feats), b...  0.71 us

profile of v3, /device:TPU:0, one launch (start us, length us, event | category | flops | bytes accessed | tf_op | source)
XLA Modules:
  0.0 22.4 jit_solution(11880011132732161773)
XLA Ops:
  0.6 21.0 %shard_map.128 = (bf16[128,128]{1,0:T(8,128)(2,1)S(1)}, bf16[128,128]{1,0:T(8,128)(2,1)S(1)}, bf16[128,128]{1,0:T(8,128)(2,1)S(1)}, bf16[128,128]{1,0:T(8,128)(2,1)S(1)}, bf16[128,128]{1,0:T(8,128)(2,1)S(1)}) custom-call(bf16[128,128]{1,0:T(8,128)(2,1)} %q_in.1, bf16[128,128]{1,0:T(8,128)(2,1)} %k_in.1, bf16[128,128]{1,0:T(8,128)(2,1)} %v_in.1, ...), custom_call_target="tpu_custom_call" | custom-call | tf_op jit(solution)/shard_map/pallas_call | solution.py:400
  21.7 0.7 %shard_map.129 = (bf16[128,128]{1,0:T(8,128)(2,1)}, bf16[128,128]{1,0:T(8,128)(2,1)}, bf16[128,128]{1,0:T(8,128)(2,1)}, bf16[128,128]{1,0:T(8,128)(2,1)}, bf16[128,128]{1,0:T(8,128)(2,1)}) custom-call(bf16[128,128]{1,0:T(8,128)(2,1)S(1)} %get-tuple-element.10.refs_0_, bf16[128,128]{1,0:T(8,128)(2,1)S(1)} %get-tuple-element.11.refs_1_, ...), custom_call_target="tpu_custom_call" | custom-call | tf_op jit(solution)/shard_map/pallas_call | solution.py:443

commit v4 on v3

--- a/solution.py
+++ b/solution.py
@@ -89,13 +89,13 @@
         pl.when(me >= d)(body)
 
     pairs = (
+        (k_in, kbuf.at[0]),
+        (v_in, vbuf.at[0]),
         (gaps_in, gaps_ref),
         (table_in, table_ref),
         (lists_in, lists_ref),
         (gain_in, gain_ref),
-        (k_in, kbuf.at[0]),
         (q_in, qbuf.at[0]),
-        (v_in, vbuf.at[0]),
         (gate_in, gate_ref),
         (cot_in, cot_ref),
     )
@@ -118,6 +118,8 @@
         jnp.minimum(me, reach) + jnp.minimum(groups - 1 - me, reach) + head_devices - 1,
     )
 
+    other_group = lax.rem(me + 1, groups)
+
     def remote(src, dst, send, recv, axis, where):
         return pltpu.make_async_remote_copy(
             src_ref=src,
@@ -138,23 +140,63 @@
             gaps_in, glater.at[k - 1], gap_send.at[1, k - 1], gap_recv.at[1, k - 1], "seq", me - k
         )
 
-    def keys_up(s):
+    def block_copy(buf, which, source, s, where):
         return remote(
-            k_in, kbuf.at[s + 1], kv_send.at[0, s], kv_recv.at[0, s], "seq", me + offsets[s]
-        )
-
-    def values_up(s):
-        return remote(
-            v_in, vbuf.at[s + 1], kv_send.at[1, s], kv_recv.at[1, s], "seq", me + offsets[s]
-        )
+            buf.at[source],
+            buf.at[s + 1],
+            kv_send.at[which, s],
+            kv_recv.at[which, s],
+            "seq",
+            where,
+        )
+
+    def pass_up(which, source, s, where):
+        block_copy((kbuf, vbuf)[which], which, source, s, where).start()
+
+    def first_up(which):
+        near = (me % 2 == 0) & (me + 1 < groups)
+        if count > 1:
+            pl.when(me + 2 < groups)(lambda: pass_up(which, 0, 1, me + 2))
+        pl.when(near)(lambda: pass_up(which, 0, 0, me + 1))
+
+    def relay_up(which, s):
+        if s == 1:
+            pl.when((me % 2 == 1) & (me >= 2))(lambda: pass_up(which, 2, 0, me - 1))
+        if 1 <= s < count - 1:
+            step = offsets[s]
+            pl.when((me >= step) & (me + step < groups))(
+                lambda: pass_up(which, s + 1, s + 1, me + step)
+            )
+
+    def wait_block(which, s):
+        block_copy((kbuf, vbuf)[which], which, 0, s, other_group).wait_recv()
+
+    def wait_block_sent(which, s):
+        block_copy((kbuf, vbuf)[which], which, 0, s, other_group).wait_send()
 
     def queries_down(s):
         return remote(q_in, qbuf.at[s + 1], q_send.at[s], q_recv.at[s], "seq", me - offsets[s])
 
-    def grads_down(s):
+    def grads_copy(source, s, where):
         return remote(
-            gabuf.at[0], gabuf.at[s + 1], ga_send.at[s], ga_recv.at[s], "seq", me - offsets[s]
-        )
+            gabuf.at[source], gabuf.at[s + 1], ga_send.at[s], ga_recv.at[s], "seq", where
+        )
+
+    def first_down():
+        if count > 1:
+            pl.when(me >= 2)(lambda: grads_copy(0, 1, me - 2).start())
+        pl.when(me % 2 == 1)(lambda: grads_copy(0, 0, me - 1).start())
+
+    def relay_down(s):
+        if s == 1:
+            pl.when((me % 2 == 0) & (me + 2 < groups))(
+                lambda: grads_copy(2, 0, me + 1).start()
+            )
+        if 1 <= s < count - 1:
+            step = offsets[s]
+            pl.when((me >= step) & (me + step < groups))(
+                lambda: grads_copy(s + 1, s + 1, me - step).start()
+            )
 
     def sums_to(r):
         return remote(
@@ -169,9 +211,11 @@
     for k in range(1, reach + 1):
         to_later(k, lambda k=k: gaps_up(k).start())
         to_earlier(k, lambda k=k: gaps_down(k).start())
+    own[0].wait()
+    own[1].wait()
+    first_up(0)
+    first_up(1)
     for s in range(count):
-        to_later(offsets[s], lambda s=s: keys_up(s).start())
-        to_later(offsets[s], lambda s=s: values_up(s).start())
         to_earlier(offsets[s], lambda s=s: queries_down(s).start())
 
     for k in range(1, reach + 1):
@@ -231,7 +275,7 @@
         slope = sig + weights * (1.0 - sig)
         return (weights * mask).astype(bf16), slope * mask
 
-    for copy in own:
+    for copy in own[2:]:
         copy.wait()
     own_gaps = gaps_ref[...].astype(f32)
     own_total = jnp.sum(own_gaps, axis=1, keepdims=True)
@@ -250,6 +294,15 @@
     diag_weights, diag_slope = activate(keys, queries, diag_bias, diag_mask)
     att_acc[...] = mm(values.T, diag_weights)
 
+    def receive(s):
+        for which in range(2):
+
+            def arrived(which=which):
+                wait_block(which, s)
+                relay_up(which, s)
+
+            to_earlier(offsets[s], arrived)
+
     for k in range(1, reach + 1):
         to_earlier(k, lambda k=k: gaps_up(k).wait_recv())
         to_later(k, lambda k=k: gaps_down(k).wait_recv())
@@ -265,6 +318,9 @@
     for s, d in enumerate(offsets):
         after = after_column(gprev[d - 1].astype(f32))
         biases.append(bias(own_row + after + between(gprev, d)))
+    if count > 1:
+        receive(1)
+
     for s, d in enumerate(offsets):
 
         def score_later(s=s, d=d):
@@ -278,14 +334,16 @@
 
         to_later(d, score_later)
 
-    for s, d in enumerate(offsets):
+    order = [s for s in (1, 0) if s < count] + list(range(2, count))
+    for s in order:
+        d = offsets[s]
+        if s != 1:
+            receive(s)
 
         def attend(s=s):
-            keys_up(s).wait_recv()
             listed = (lists_ref[me, s] >= 0).astype(f32)
             weights, slope = activate(kbuf[s + 1], queries, biases[s], listed)
             slope_q[s] = slope
-            values_up(s).wait_recv()
             att_acc[...] += mm(vbuf[s + 1].T, weights)
 
         to_earlier(d, attend)
@@ -311,8 +369,7 @@
     product_mean = inv_std * (sums[3:4] - mean * sums[2:3]) / full_width
     grad = (inv_std * (scaled - scaled_mean - centered * product_mean)).astype(bf16)
     gabuf[0] = grad
-    for s in range(count):
-        to_earlier(offsets[s], lambda s=s: grads_down(s).start())
+    first_down()
 
     grads = by_head_lanes(grad)
     diag_grad = (mm(values, grads) * diag_slope).astype(bf16)
@@ -326,15 +383,26 @@
             dq_acc[...] += mm(kbuf[s + 1].T, grad_scores)
 
         to_earlier(d, query_part)
+    def receive_grads(s):
+        def arrived():
+            grads_copy(0, s, other_group).wait_recv()
+            relay_down(s)
+
+        to_later(offsets[s], arrived)
+
+    if count > 1:
+        receive_grads(1)
     dq_ref[...] = (own_heads(dq_acc[...]) * scaling).T.astype(bf16)
     normed = centered.T * gain
     layer_ref[...] = (normed * gates).astype(bf16)
     dgate_ref[...] = (upstream * normed).astype(bf16)
 
-    for s, d in enumerate(offsets):
+    for s in order:
+        d = offsets[s]
+        if s != 1:
+            receive_grads(s)
 
         def key_part(s=s):
-            grads_down(s).wait_recv()
             grads = by_head_lanes(gabuf[s + 1])
             grad_scores = (mm(values, grads) * slope_k[s]).astype(bf16)
             dk_acc[...] += mm(grad_scores, by_head_rows(qbuf[s + 1]))
@@ -348,10 +416,19 @@
         to_later(k, lambda k=k: gaps_up(k).wait_send())
         to_earlier(k, lambda k=k: gaps_down(k).wait_send())
     for s, d in enumerate(offsets):
-        to_later(d, lambda s=s: keys_up(s).wait_send())
-        to_later(d, lambda s=s: values_up(s).wait_send())
+        if s == 0:
+            sent_up = ((me % 2 == 0) & (me + 1 < groups)) | ((me % 2 == 1) & (me >= 2))
+            sent_down = (me % 2 == 1) | ((me % 2 == 0) & (me + 2 < groups))
+        elif s == 1:
+            sent_up = me + 2 < groups
+            sent_down = me >= 2
+        else:
+            sent_up = (me >= d // 2) & (me + d // 2 < groups)
+            sent_down = sent_up
+        for which in range(2):
+            pl.when(sent_up)(lambda which=which, s=s: wait_block_sent(which, s))
         to_earlier(d, lambda s=s: queries_down(s).wait_send())
-        to_earlier(d, lambda s=s: grads_down(s).wait_send())
+        pl.when(sent_down)(lambda s=s: grads_copy(0, s, other_group).wait_send())
     for r in range(1, head_devices):
         sums_to(r).wait_send()
 

time: 22.5 us -> 23.8 us (1.058)
  Pallas kernels: 21.7 us -> 23 us
    pallas_call x1, Pallas kernels: 21 us -> 22.3 us  [per_device(): pl.pallas_call(functools.partial(kernel, groups, head_devices, offsets),...]
where the time goes in v4:
time: 23.8 us; the launch traced here: 23.7 us
  Pallas kernels  23 us (97%)
  between operations  0.64 us (3%)
    pallas_call x1, Pallas kernels, per_device(): pl.pallas_call(functools.partial(kernel, groups, head_devices, offsets),...  22.3 us
    pallas_call x1, Pallas kernels, per_device(): pl.pallas_call(hand_out, out_shape=[jax.ShapeDtypeStruct((rows, feats), b...  0.71 us

profile of v4, /device:TPU:0, one launch (start us, length us, event | category | flops | bytes accessed | tf_op | source)
XLA Modules:
  0.0 23.7 jit_solution(6953097394081368851)
XLA Ops:
  0.6 22.3 %shard_map.128 = (bf16[128,128]{1,0:T(8,128)(2,1)S(1)}, bf16[128,128]{1,0:T(8,128)(2,1)S(1)}, bf16[128,128]{1,0:T(8,128)(2,1)S(1)}, bf16[128,128]{1,0:T(8,128)(2,1)S(1)}, bf16[128,128]{1,0:T(8,128)(2,1)S(1)}) custom-call(bf16[128,128]{1,0:T(8,128)(2,1)} %q_in.1, bf16[128,128]{1,0:T(8,128)(2,1)} %k_in.1, bf16[128,128]{1,0:T(8,128)(2,1)} %v_in.1, ...), custom_call_target="tpu_custom_call" | custom-call | tf_op jit(solution)/shard_map/pallas_call | solution.py:477
  23.0 0.7 %shard_map.129 = (bf16[128,128]{1,0:T(8,128)(2,1)}, bf16[128,128]{1,0:T(8,128)(2,1)}, bf16[128,128]{1,0:T(8,128)(2,1)}, bf16[128,128]{1,0:T(8,128)(2,1)}, bf16[128,128]{1,0:T(8,128)(2,1)}) custom-call(bf16[128,128]{1,0:T(8,128)(2,1)S(1)} %get-tuple-element.10.refs_0_, bf16[128,128]{1,0:T(8,128)(2,1)S(1)} %get-tuple-element.11.refs_1_, ...), custom_call_target="tpu_custom_call" | custom-call | tf_op jit(solution)/shard_map/pallas_call | solution.py:520

commit v5 on v4

--- a/solution.py
+++ b/solution.py
@@ -177,26 +177,10 @@
     def queries_down(s):
         return remote(q_in, qbuf.at[s + 1], q_send.at[s], q_recv.at[s], "seq", me - offsets[s])
 
-    def grads_copy(source, s, where):
+    def grads_down(s):
         return remote(
-            gabuf.at[source], gabuf.at[s + 1], ga_send.at[s], ga_recv.at[s], "seq", where
-        )
-
-    def first_down():
-        if count > 1:
-            pl.when(me >= 2)(lambda: grads_copy(0, 1, me - 2).start())
-        pl.when(me % 2 == 1)(lambda: grads_copy(0, 0, me - 1).start())
-
-    def relay_down(s):
-        if s == 1:
-            pl.when((me % 2 == 0) & (me + 2 < groups))(
-                lambda: grads_copy(2, 0, me + 1).start()
-            )
-        if 1 <= s < count - 1:
-            step = offsets[s]
-            pl.when((me >= step) & (me + step < groups))(
-                lambda: grads_copy(s + 1, s + 1, me - step).start()
-            )
+            gabuf.at[0], gabuf.at[s + 1], ga_send.at[s], ga_recv.at[s], "seq", me - offsets[s]
+        )
 
     def sums_to(r):
         return remote(
@@ -369,7 +353,8 @@
     product_mean = inv_std * (sums[3:4] - mean * sums[2:3]) / full_width
     grad = (inv_std * (scaled - scaled_mean - centered * product_mean)).astype(bf16)
     gabuf[0] = grad
-    first_down()
+    for s in range(count):
+        to_earlier(offsets[s], lambda s=s: grads_down(s).start())
 
     grads = by_head_lanes(grad)
     diag_grad = (mm(values, grads) * diag_slope).astype(bf16)
@@ -383,26 +368,15 @@
             dq_acc[...] += mm(kbuf[s + 1].T, grad_scores)
 
         to_earlier(d, query_part)
-    def receive_grads(s):
-        def arrived():
-            grads_copy(0, s, other_group).wait_recv()
-            relay_down(s)
-
-        to_later(offsets[s], arrived)
-
-    if count > 1:
-        receive_grads(1)
     dq_ref[...] = (own_heads(dq_acc[...]) * scaling).T.astype(bf16)
     normed = centered.T * gain
     layer_ref[...] = (normed * gates).astype(bf16)
     dgate_ref[...] = (upstream * normed).astype(bf16)
 
-    for s in order:
-        d = offsets[s]
-        if s != 1:
-            receive_grads(s)
+    for s, d in enumerate(offsets):
 
         def key_part(s=s):
+            grads_down(s).wait_recv()
             grads = by_head_lanes(gabuf[s + 1])
             grad_scores = (mm(values, grads) * slope_k[s]).astype(bf16)
             dk_acc[...] += mm(grad_scores, by_head_rows(qbuf[s + 1]))
@@ -418,17 +392,14 @@
     for s, d in enumerate(offsets):
         if s == 0:
             sent_up = ((me % 2 == 0) & (me + 1 < groups)) | ((me % 2 == 1) & (me >= 2))
-            sent_down = (me % 2 == 1) | ((me % 2 == 0) & (me + 2 < groups))
         elif s == 1:
             sent_up = me + 2 < groups
-            sent_down = me >= 2
         else:
             sent_up = (me >= d // 2) & (me + d // 2 < groups)
-            sent_down = sent_up
         for which in range(2):
             pl.when(sent_up)(lambda which=which, s=s: wait_block_sent(which, s))
         to_earlier(d, lambda s=s: queries_down(s).wait_send())
-        pl.when(sent_down)(lambda s=s: grads_copy(0, s, other_group).wait_send())
+        to_earlier(d, lambda s=s: grads_down(s).wait_send())
     for r in range(1, head_devices):
         sums_to(r).wait_send()
 

time: 23.8 us -> 22.8 us (0.958)
  Pallas kernels: 23 us -> 22 us
    pallas_call x1, Pallas kernels: 22.3 us -> 21.3 us  [per_device(): pl.pallas_call(functools.partial(kernel, groups, head_devices, offsets),...]
where the time goes in v5:
time: 22.8 us; the launch traced here: 22.7 us
  Pallas kernels  22 us (96%)
  between operations  0.64 us (3%)
    pallas_call x1, Pallas kernels, per_device(): pl.pallas_call(functools.partial(kernel, groups, head_devices, offsets),...  21.3 us
    pallas_call x1, Pallas kernels, per_device(): pl.pallas_call(hand_out, out_shape=[jax.ShapeDtypeStruct((rows, feats), b...  0.71 us

profile of v5, /device:TPU:0, one launch (start us, length us, event | category | flops | bytes accessed | tf_op | source)
XLA Modules:
  0.0 22.7 jit_solution(10016475085021843821)
XLA Ops:
  0.6 21.3 %shard_map.128 = (bf16[128,128]{1,0:T(8,128)(2,1)S(1)}, bf16[128,128]{1,0:T(8,128)(2,1)S(1)}, bf16[128,128]{1,0:T(8,128)(2,1)S(1)}, bf16[128,128]{1,0:T(8,128)(2,1)S(1)}, bf16[128,128]{1,0:T(8,128)(2,1)S(1)}) custom-call(bf16[128,128]{1,0:T(8,128)(2,1)} %q_in.1, bf16[128,128]{1,0:T(8,128)(2,1)} %k_in.1, bf16[128,128]{1,0:T(8,128)(2,1)} %v_in.1, ...), custom_call_target="tpu_custom_call" | custom-call | tf_op jit(solution)/shard_map/pallas_call | solution.py:448
  21.9 0.7 %shard_map.129 = (bf16[128,128]{1,0:T(8,128)(2,1)}, bf16[128,128]{1,0:T(8,128)(2,1)}, bf16[128,128]{1,0:T(8,128)(2,1)}, bf16[128,128]{1,0:T(8,128)(2,1)}, bf16[128,128]{1,0:T(8,128)(2,1)}) custom-call(bf16[128,128]{1,0:T(8,128)(2,1)S(1)} %get-tuple-element.10.refs_0_, bf16[128,128]{1,0:T(8,128)(2,1)S(1)} %get-tuple-element.11.refs_1_, ...), custom_call_target="tpu_custom_call" | custom-call | tf_op jit(solution)/shard_map/pallas_call | solution.py:491

commit v6 on v3

--- a/solution.py
+++ b/solution.py
@@ -56,10 +56,6 @@
     slope_q,
     slope_k,
     weight_k,
-    att_acc,
-    dq_acc,
-    dk_acc,
-    dv_acc,
     local_sem,
     gap_send,
     gap_recv,
@@ -184,6 +180,18 @@
 
         pl.when(me < k)(no_earlier)
         pl.when(me + k >= groups)(no_later)
+    for s, d in enumerate(offsets):
+
+        def no_keys(s=s):
+            kbuf[s + 1] = jnp.zeros((rows, feats), bf16)
+            vbuf[s + 1] = jnp.zeros((rows, feats), bf16)
+
+        def no_queries(s=s):
+            qbuf[s + 1] = jnp.zeros((rows, feats), bf16)
+            gabuf[s + 1] = jnp.zeros((feats, rows), bf16)
+
+        pl.when(me < d)(no_keys)
+        pl.when(me + d >= groups)(no_queries)
 
     row_ids = lax.broadcasted_iota(jnp.int32, (rows, rows), 0)
     col_ids = lax.broadcasted_iota(jnp.int32, (rows, rows), 1)
@@ -203,11 +211,11 @@
         return mm(jnp.where(col_ids > row_ids, gaps, 0.0).astype(bf16), ones)
 
     def bias(delta):
-        parts = [jnp.full(delta.shape, table_ref[h, 0], f32) for h in range(heads)]
-        for b in range(1, buckets):
-            reached = delta >= float(2 ** (b - 1))
-            parts = [jnp.where(reached, table_ref[h, b], parts[h]) for h in range(heads)]
-        return jnp.concatenate(parts, axis=1)
+        whole = jnp.maximum(delta, 0.0).astype(jnp.int32)
+        bucket = jnp.minimum(32 - lax.clz(whole), buckets - 1)
+        return jnp.concatenate(
+            [jnp.take_along_axis(table, bucket, axis=1) for table in tables], axis=1
+        )
 
     def by_head_rows(q):
         return jnp.concatenate([q * mask for mask in lane_masks], axis=0)
@@ -224,8 +232,8 @@
             axis=0,
         )
 
-    def activate(keys, queries, biases, mask):
-        scores = mm_nt(keys, queries) * scaling + biases
+    def activate(products, biases, mask):
+        scores = products * scaling + biases
         sig = 0.5 * jnp.tanh(0.5 * scores) + 0.5
         weights = scores * sig
         slope = sig + weights * (1.0 - sig)
@@ -233,6 +241,13 @@
 
     for copy in own:
         copy.wait()
+    lanes = lax.broadcasted_iota(jnp.int32, (rows, rows), 1)
+    tables = []
+    for h in range(heads):
+        table = jnp.zeros((rows, rows), f32)
+        for b in range(buckets):
+            table = jnp.where(lanes == b, table_ref[h, b], table)
+        tables.append(table)
     own_gaps = gaps_ref[...].astype(f32)
     own_total = jnp.sum(own_gaps, axis=1, keepdims=True)
     own_row = prefix_row(own_gaps)
@@ -247,8 +262,8 @@
     keys = kbuf[0]
     values = vbuf[0]
     queries = by_head_rows(qbuf[0])
-    diag_weights, diag_slope = activate(keys, queries, diag_bias, diag_mask)
-    att_acc[...] = mm(values.T, diag_weights)
+    diag_weights, diag_slope = activate(mm_nt(keys, queries), diag_bias, diag_mask)
+    attended = mm(values.T, diag_weights)
 
     for k in range(1, reach + 1):
         to_earlier(k, lambda k=k: gaps_up(k).wait_recv())
@@ -266,37 +281,42 @@
         after = after_column(gprev[d - 1].astype(f32))
         biases.append(bias(own_row + after + between(gprev, d)))
     for s, d in enumerate(offsets):
-
-        def score_later(s=s, d=d):
-            row = prefix_row(glater[d - 1].astype(f32))
-            later_bias = bias(row + own_after + between(glater, d))
-            listed = (lists_ref[me + d, s] >= 0).astype(f32)
-            queries_down(s).wait_recv()
-            weights, slope = activate(keys, by_head_rows(qbuf[s + 1]), later_bias, listed)
-            weight_k[s] = weights
-            slope_k[s] = slope
-
-        to_later(d, score_later)
-
-    for s, d in enumerate(offsets):
-
-        def attend(s=s):
-            keys_up(s).wait_recv()
-            listed = (lists_ref[me, s] >= 0).astype(f32)
-            weights, slope = activate(kbuf[s + 1], queries, biases[s], listed)
-            slope_q[s] = slope
-            values_up(s).wait_recv()
-            att_acc[...] += mm(vbuf[s + 1].T, weights)
-
-        to_earlier(d, attend)
-
-    flat = own_heads(att_acc[...])
+        to_earlier(d, lambda s=s: keys_up(s).wait_recv())
+        to_earlier(d, lambda s=s: values_up(s).wait_recv())
+    early_keys = kbuf[1 : count + 1].reshape(count * rows, feats)
+    early_values = vbuf[1 : count + 1].reshape(count * rows, feats)
+    early_scores = mm_nt(early_keys, queries)
+    early_weights = []
+    for s in range(count):
+        listed = (lists_ref[me, s] >= 0).astype(f32)
+        part = early_scores[s * rows : (s + 1) * rows]
+        weights, slope = activate(part, biases[s], listed)
+        slope_q[s] = slope
+        early_weights.append(weights)
+    attended = attended + mm(early_values.T, jnp.concatenate(early_weights, axis=0))
+
+    flat = own_heads(attended)
     own_sums = [
         jnp.sum(x, axis=0, keepdims=True) for x in (flat, flat * flat, scaled, scaled * flat)
     ]
     sums_out[...] = jnp.concatenate(own_sums + [jnp.zeros((4, rows), f32)], axis=0)
     for r in range(1, head_devices):
         sums_to(r).start()
+
+    for s, d in enumerate(offsets):
+        to_later(d, lambda s=s: queries_down(s).wait_recv())
+    late_queries = jnp.concatenate([by_head_rows(qbuf[s + 1]) for s in range(count)], axis=0)
+    late_scores = mm_nt(keys, late_queries)
+    wide = heads * rows
+    for s, d in enumerate(offsets):
+        row = prefix_row(glater[d - 1].astype(f32))
+        later_bias = bias(row + own_after + between(glater, d))
+        there = jnp.minimum(me + d, groups - 1)
+        listed = ((lists_ref[there, s] >= 0) & (me + d < groups)).astype(f32)
+        part = late_scores[:, s * wide : (s + 1) * wide]
+        weights, slope = activate(part, later_bias, listed)
+        weight_k[:, s * wide : (s + 1) * wide] = weights
+        slope_k[:, s * wide : (s + 1) * wide] = slope
 
     for r in range(1, head_devices):
         sums_to(r).wait_recv()
@@ -316,33 +336,30 @@
 
     grads = by_head_lanes(grad)
     diag_grad = (mm(values, grads) * diag_slope).astype(bf16)
-    dq_acc[...] = mm(keys.T, diag_grad)
-    dk_acc[...] = mm(diag_grad, queries)
-    dv_acc[...] = mm_nt(diag_weights, grads)
-    for s, d in enumerate(offsets):
-
-        def query_part(s=s):
-            grad_scores = (mm(vbuf[s + 1], grads) * slope_q[s]).astype(bf16)
-            dq_acc[...] += mm(kbuf[s + 1].T, grad_scores)
-
-        to_earlier(d, query_part)
-    dq_ref[...] = (own_heads(dq_acc[...]) * scaling).T.astype(bf16)
+    early_products = mm(early_values, grads)
+    grad_scores = jnp.concatenate(
+        [
+            (early_products[s * rows : (s + 1) * rows] * slope_q[s]).astype(bf16)
+            for s in range(count)
+        ],
+        axis=0,
+    )
+    dq = mm(keys.T, diag_grad) + mm(early_keys.T, grad_scores)
+    dk = mm(diag_grad, queries)
+    dv = mm_nt(diag_weights, grads)
+    dq_ref[...] = (own_heads(dq) * scaling).T.astype(bf16)
     normed = centered.T * gain
     layer_ref[...] = (normed * gates).astype(bf16)
     dgate_ref[...] = (upstream * normed).astype(bf16)
 
     for s, d in enumerate(offsets):
-
-        def key_part(s=s):
-            grads_down(s).wait_recv()
-            grads = by_head_lanes(gabuf[s + 1])
-            grad_scores = (mm(values, grads) * slope_k[s]).astype(bf16)
-            dk_acc[...] += mm(grad_scores, by_head_rows(qbuf[s + 1]))
-            dv_acc[...] += mm_nt(weight_k[s], grads)
-
-        to_later(d, key_part)
-    dk_ref[...] = (dk_acc[...] * scaling).astype(bf16)
-    dv_ref[...] = dv_acc[...].astype(bf16)
+        to_later(d, lambda s=s: grads_down(s).wait_recv())
+    late_grads = jnp.concatenate([by_head_lanes(gabuf[s + 1]) for s in range(count)], axis=1)
+    late_products = (mm(values, late_grads) * slope_k[...]).astype(bf16)
+    dk = dk + mm(late_products, late_queries)
+    dv = dv + mm_nt(weight_k[...], late_grads)
+    dk_ref[...] = (dk * scaling).astype(bf16)
+    dv_ref[...] = dv.astype(bf16)
 
     for k in range(1, reach + 1):
         to_later(k, lambda k=k: gaps_up(k).wait_send())
@@ -418,12 +435,8 @@
             pltpu.VMEM((8, rows), f32),
             pltpu.VMEM((head_devices - 1, 8, rows), f32),
             pltpu.VMEM((count, rows, heads * rows), f32),
-            pltpu.VMEM((count, rows, heads * rows), f32),
-            pltpu.VMEM((count, rows, heads * rows), bf16),
-            pltpu.VMEM((feats, heads * rows), f32),
-            pltpu.VMEM((feats, heads * rows), f32),
-            pltpu.VMEM((rows, feats), f32),
-            pltpu.VMEM((rows, feats), f32),
+            pltpu.VMEM((rows, count * heads * rows), f32),
+            pltpu.VMEM((rows, count * heads * rows), bf16),
             dma((9,)),
             dma((2, reach)),
             dma((2, reach)),

time: 22.5 us -> 21.7 us (0.964)
  Pallas kernels: 21.7 us -> 20.9 us
    pallas_call x1, Pallas kernels: 21 us -> 20.2 us  [per_device(): pl.pallas_call(functools.partial(kernel, groups, head_devices, offsets),...]
where the time goes in v6:
time: 21.7 us; the launch traced here: 21.5 us
  Pallas kernels  20.9 us (96%)
  between operations  0.64 us (3%)
    pallas_call x1, Pallas kernels, per_device(): pl.pallas_call(functools.partial(kernel, groups, head_devices, offsets),...  20.2 us
    pallas_call x1, Pallas kernels, per_device(): pl.pallas_call(hand_out, out_shape=[jax.ShapeDtypeStruct((rows, feats), b...  0.71 us

profile of v6, /device:TPU:0, one launch (start us, length us, event | category | flops | bytes accessed | tf_op | source)
XLA Modules:
  0.0 21.5 jit_solution(15646358696227610844)
XLA Ops:
  0.6 20.2 %shard_map.128 = (bf16[128,128]{1,0:T(8,128)(2,1)S(1)}, bf16[128,128]{1,0:T(8,128)(2,1)S(1)}, bf16[128,128]{1,0:T(8,128)(2,1)S(1)}, bf16[128,128]{1,0:T(8,128)(2,1)S(1)}, bf16[128,128]{1,0:T(8,128)(2,1)S(1)}) custom-call(bf16[128,128]{1,0:T(8,128)(2,1)} %q_in.1, bf16[128,128]{1,0:T(8,128)(2,1)} %k_in.1, bf16[128,128]{1,0:T(8,128)(2,1)} %v_in.1, ...), custom_call_target="tpu_custom_call" | custom-call | tf_op jit(solution)/shard_map/pallas_call | solution.py:417
  20.8 0.7 %shard_map.129 = (bf16[128,128]{1,0:T(8,128)(2,1)}, bf16[128,128]{1,0:T(8,128)(2,1)}, bf16[128,128]{1,0:T(8,128)(2,1)}, bf16[128,128]{1,0:T(8,128)(2,1)}, bf16[128,128]{1,0:T(8,128)(2,1)}) custom-call(bf16[128,128]{1,0:T(8,128)(2,1)S(1)} %get-tuple-element.10.refs_0_, bf16[128,128]{1,0:T(8,128)(2,1)S(1)} %get-tuple-element.11.refs_1_, ...), custom_call_target="tpu_custom_call" | custom-call | tf_op jit(solution)/shard_map/pallas_call | solution.py:456

commit v7 on v6

--- a/solution.py
+++ b/solution.py
@@ -85,13 +85,13 @@
         pl.when(me >= d)(body)
 
     pairs = (
+        (k_in, kbuf.at[0]),
+        (v_in, vbuf.at[0]),
         (gaps_in, gaps_ref),
         (table_in, table_ref),
         (lists_in, lists_ref),
         (gain_in, gain_ref),
-        (k_in, kbuf.at[0]),
         (q_in, qbuf.at[0]),
-        (v_in, vbuf.at[0]),
         (gate_in, gate_ref),
         (cot_in, cot_ref),
     )
@@ -114,6 +114,8 @@
         jnp.minimum(me, reach) + jnp.minimum(groups - 1 - me, reach) + head_devices - 1,
     )
 
+    other_group = lax.rem(me + 1, groups)
+
     def remote(src, dst, send, recv, axis, where):
         return pltpu.make_async_remote_copy(
             src_ref=src,
@@ -134,15 +136,39 @@
             gaps_in, glater.at[k - 1], gap_send.at[1, k - 1], gap_recv.at[1, k - 1], "seq", me - k
         )
 
-    def keys_up(s):
+    def block_copy(buf, which, source, s, where):
         return remote(
-            k_in, kbuf.at[s + 1], kv_send.at[0, s], kv_recv.at[0, s], "seq", me + offsets[s]
-        )
-
-    def values_up(s):
-        return remote(
-            v_in, vbuf.at[s + 1], kv_send.at[1, s], kv_recv.at[1, s], "seq", me + offsets[s]
-        )
+            buf.at[source],
+            buf.at[s + 1],
+            kv_send.at[which, s],
+            kv_recv.at[which, s],
+            "seq",
+            where,
+        )
+
+    def pass_up(which, source, s, where):
+        block_copy((kbuf, vbuf)[which], which, source, s, where).start()
+
+    def first_up(which):
+        near = (me % 2 == 0) & (me + 1 < groups)
+        if count > 1:
+            pl.when(me + 2 < groups)(lambda: pass_up(which, 0, 1, me + 2))
+        pl.when(near)(lambda: pass_up(which, 0, 0, me + 1))
+
+    def relay_up(which, s):
+        if s == 1:
+            pl.when((me % 2 == 1) & (me >= 2))(lambda: pass_up(which, 2, 0, me - 1))
+        if 1 <= s < count - 1:
+            step = offsets[s]
+            pl.when((me >= step) & (me + step < groups))(
+                lambda: pass_up(which, s + 1, s + 1, me + step)
+            )
+
+    def wait_block(which, s):
+        block_copy((kbuf, vbuf)[which], which, 0, s, other_group).wait_recv()
+
+    def wait_block_sent(which, s):
+        block_copy((kbuf, vbuf)[which], which, 0, s, other_group).wait_send()
 
     def queries_down(s):
         return remote(q_in, qbuf.at[s + 1], q_send.at[s], q_recv.at[s], "seq", me - offsets[s])
@@ -165,9 +191,11 @@
     for k in range(1, reach + 1):
         to_later(k, lambda k=k: gaps_up(k).start())
         to_earlier(k, lambda k=k: gaps_down(k).start())
+    own[0].wait()
+    own[1].wait()
+    first_up(0)
+    first_up(1)
     for s in range(count):
-        to_later(offsets[s], lambda s=s: keys_up(s).start())
-        to_later(offsets[s], lambda s=s: values_up(s).start())
         to_earlier(offsets[s], lambda s=s: queries_down(s).start())
 
     for k in range(1, reach + 1):
@@ -239,7 +267,7 @@
         slope = sig + weights * (1.0 - sig)
         return (weights * mask).astype(bf16), slope * mask
 
-    for copy in own:
+    for copy in own[2:]:
         copy.wait()
     lanes = lax.broadcasted_iota(jnp.int32, (rows, rows), 1)
     tables = []
@@ -280,9 +308,17 @@
     for s, d in enumerate(offsets):
         after = after_column(gprev[d - 1].astype(f32))
         biases.append(bias(own_row + after + between(gprev, d)))
-    for s, d in enumerate(offsets):
-        to_earlier(d, lambda s=s: keys_up(s).wait_recv())
-        to_earlier(d, lambda s=s: values_up(s).wait_recv())
+    def receive(s):
+        for which in range(2):
+
+            def arrived(which=which):
+                wait_block(which, s)
+                relay_up(which, s)
+
+            to_earlier(offsets[s], arrived)
+
+    for s in [s for s in (1, 0) if s < count] + list(range(2, count)):
+        receive(s)
     early_keys = kbuf[1 : count + 1].reshape(count * rows, feats)
     early_values = vbuf[1 : count + 1].reshape(count * rows, feats)
     early_scores = mm_nt(early_keys, queries)
@@ -365,8 +401,14 @@
         to_later(k, lambda k=k: gaps_up(k).wait_send())
         to_earlier(k, lambda k=k: gaps_down(k).wait_send())
     for s, d in enumerate(offsets):
-        to_later(d, lambda s=s: keys_up(s).wait_send())
-        to_later(d, lambda s=s: values_up(s).wait_send())
+        if s == 0:
+            sent_up = ((me % 2 == 0) & (me + 1 < groups)) | ((me % 2 == 1) & (me >= 2))
+        elif s == 1:
+            sent_up = me + 2 < groups
+        else:
+            sent_up = (me >= d // 2) & (me + d // 2 < groups)
+        for which in range(2):
+            pl.when(sent_up)(lambda which=which, s=s: wait_block_sent(which, s))
         to_earlier(d, lambda s=s: queries_down(s).wait_send())
         to_earlier(d, lambda s=s: grads_down(s).wait_send())
     for r in range(1, head_devices):

time: 21.7 us -> 22.7 us (1.046)
  Pallas kernels: 20.9 us -> 22 us
    pallas_call x1, Pallas kernels: 20.2 us -> 21.2 us  [per_device(): pl.pallas_call(functools.partial(kernel, groups, head_devices, offsets),...]
where the time goes in v7:
time: 22.7 us; the launch traced here: 22.6 us
  Pallas kernels  22 us (97%)
  between operations  0.64 us (3%)
    pallas_call x1, Pallas kernels, per_device(): pl.pallas_call(functools.partial(kernel, groups, head_devices, offsets),...  21.2 us
    pallas_call x1, Pallas kernels, per_device(): pl.pallas_call(hand_out, out_shape=[jax.ShapeDtypeStruct((rows, feats), b...  0.71 us

profile of v7, /device:TPU:0, one launch (start us, length us, event | category | flops | bytes accessed | tf_op | source)
XLA Modules:
  0.0 22.6 jit_solution(14595055913772456931)
XLA Ops:
  0.6 21.2 %shard_map.128 = (bf16[128,128]{1,0:T(8,128)(2,1)S(1)}, bf16[128,128]{1,0:T(8,128)(2,1)S(1)}, bf16[128,128]{1,0:T(8,128)(2,1)S(1)}, bf16[128,128]{1,0:T(8,128)(2,1)S(1)}, bf16[128,128]{1,0:T(8,128)(2,1)S(1)}) custom-call(bf16[128,128]{1,0:T(8,128)(2,1)} %q_in.1, bf16[128,128]{1,0:T(8,128)(2,1)} %k_in.1, bf16[128,128]{1,0:T(8,128)(2,1)} %v_in.1, ...), custom_call_target="tpu_custom_call" | custom-call | tf_op jit(solution)/shard_map/pallas_call | solution.py:459
  21.9 0.7 %shard_map.129 = (bf16[128,128]{1,0:T(8,128)(2,1)}, bf16[128,128]{1,0:T(8,128)(2,1)}, bf16[128,128]{1,0:T(8,128)(2,1)}, bf16[128,128]{1,0:T(8,128)(2,1)}, bf16[128,128]{1,0:T(8,128)(2,1)}) custom-call(bf16[128,128]{1,0:T(8,128)(2,1)S(1)} %get-tuple-element.10.refs_0_, bf16[128,128]{1,0:T(8,128)(2,1)S(1)} %get-tuple-element.11.refs_1_, ...), custom_call_target="tpu_custom_call" | custom-call | tf_op jit(solution)/shard_map/pallas_call | solution.py:498

commit v8 on v6

--- a/solution.py
+++ b/solution.py
@@ -165,9 +165,10 @@
     for k in range(1, reach + 1):
         to_later(k, lambda k=k: gaps_up(k).start())
         to_earlier(k, lambda k=k: gaps_down(k).start())
-    for s in range(count):
+    for s in reversed(range(count)):
         to_later(offsets[s], lambda s=s: keys_up(s).start())
         to_later(offsets[s], lambda s=s: values_up(s).start())
+    for s in reversed(range(count)):
         to_earlier(offsets[s], lambda s=s: queries_down(s).start())
 
     for k in range(1, reach + 1):
@@ -305,6 +306,8 @@
 
     for s, d in enumerate(offsets):
         to_later(d, lambda s=s: queries_down(s).wait_recv())
+    keys_t = keys.T
+    early_keys_t = early_keys.T
     late_queries = jnp.concatenate([by_head_rows(qbuf[s + 1]) for s in range(count)], axis=0)
     late_scores = mm_nt(keys, late_queries)
     wide = heads * rows
@@ -331,7 +334,7 @@
     product_mean = inv_std * (sums[3:4] - mean * sums[2:3]) / full_width
     grad = (inv_std * (scaled - scaled_mean - centered * product_mean)).astype(bf16)
     gabuf[0] = grad
-    for s in range(count):
+    for s in reversed(range(count)):
         to_earlier(offsets[s], lambda s=s: grads_down(s).start())
 
     grads = by_head_lanes(grad)
@@ -344,7 +347,7 @@
         ],
         axis=0,
     )
-    dq = mm(keys.T, diag_grad) + mm(early_keys.T, grad_scores)
+    dq = mm(keys_t, diag_grad) + mm(early_keys_t, grad_scores)
     dk = mm(diag_grad, queries)
     dv = mm_nt(diag_weights, grads)
     dq_ref[...] = (own_heads(dq) * scaling).T.astype(bf16)

time: 21.7 us -> 22.7 us (1.046)
  Pallas kernels: 20.9 us -> 21.9 us
    pallas_call x1, Pallas kernels: 20.2 us -> 21.2 us  [per_device(): pl.pallas_call(functools.partial(kernel, groups, head_devices, offsets),...]
where the time goes in v8:
time: 22.7 us; the launch traced here: 22.5 us
  Pallas kernels  21.9 us (96%)
  between operations  0.64 us (3%)
    pallas_call x1, Pallas kernels, per_device(): pl.pallas_call(functools.partial(kernel, groups, head_devices, offsets),...  21.2 us
    pallas_call x1, Pallas kernels, per_device(): pl.pallas_call(hand_out, out_shape=[jax.ShapeDtypeStruct((rows, feats), b...  0.71 us

profile of v8, /device:TPU:0, one launch (start us, length us, event | category | flops | bytes accessed | tf_op | source)
XLA Modules:
  0.0 22.5 jit_solution(17111576151222278010)
XLA Ops:
  0.6 21.2 %shard_map.128 = (bf16[128,128]{1,0:T(8,128)(2,1)S(1)}, bf16[128,128]{1,0:T(8,128)(2,1)S(1)}, bf16[128,128]{1,0:T(8,128)(2,1)S(1)}, bf16[128,128]{1,0:T(8,128)(2,1)S(1)}, bf16[128,128]{1,0:T(8,128)(2,1)S(1)}) custom-call(bf16[128,128]{1,0:T(8,128)(2,1)} %q_in.1, bf16[128,128]{1,0:T(8,128)(2,1)} %k_in.1, bf16[128,128]{1,0:T(8,128)(2,1)} %v_in.1, ...), custom_call_target="tpu_custom_call" | custom-call | tf_op jit(solution)/shard_map/pallas_call | solution.py:420
  21.8 0.7 %shard_map.129 = (bf16[128,128]{1,0:T(8,128)(2,1)}, bf16[128,128]{1,0:T(8,128)(2,1)}, bf16[128,128]{1,0:T(8,128)(2,1)}, bf16[128,128]{1,0:T(8,128)(2,1)}, bf16[128,128]{1,0:T(8,128)(2,1)}) custom-call(bf16[128,128]{1,0:T(8,128)(2,1)S(1)} %get-tuple-element.10.refs_0_, bf16[128,128]{1,0:T(8,128)(2,1)S(1)} %get-tuple-element.11.refs_1_, ...), custom_call_target="tpu_custom_call" | custom-call | tf_op jit(solution)/shard_map/pallas_call | solution.py:459

commit v9 on v8

--- a/solution.py
+++ b/solution.py
@@ -165,10 +165,9 @@
     for k in range(1, reach + 1):
         to_later(k, lambda k=k: gaps_up(k).start())
         to_earlier(k, lambda k=k: gaps_down(k).start())
-    for s in reversed(range(count)):
+    for s in range(count):
         to_later(offsets[s], lambda s=s: keys_up(s).start())
         to_later(offsets[s], lambda s=s: values_up(s).start())
-    for s in reversed(range(count)):
         to_earlier(offsets[s], lambda s=s: queries_down(s).start())
 
     for k in range(1, reach + 1):

time: 22.7 us -> 21 us (0.925)
  Pallas kernels: 21.9 us -> 20.2 us
    pallas_call x1, Pallas kernels: 21.2 us -> 19.5 us  [per_device(): pl.pallas_call(functools.partial(kernel, groups, head_devices, offsets),...]
where the time goes in v9:
time: 21 us; the launch traced here: 20.8 us
  Pallas kernels  20.2 us (96%)
  between operations  0.64 us (3%)
    pallas_call x1, Pallas kernels, per_device(): pl.pallas_call(functools.partial(kernel, groups, head_devices, offsets),...  19.5 us
    pallas_call x1, Pallas kernels, per_device(): pl.pallas_call(hand_out, out_shape=[jax.ShapeDtypeStruct((rows, feats), b...  0.71 us

profile of v9, /device:TPU:0, one launch (start us, length us, event | category | flops | bytes accessed | tf_op | source)
XLA Modules:
  0.0 20.8 jit_solution(7039953377376287578)
XLA Ops:
  0.6 19.5 %shard_map.128 = (bf16[128,128]{1,0:T(8,128)(2,1)S(1)}, bf16[128,128]{1,0:T(8,128)(2,1)S(1)}, bf16[128,128]{1,0:T(8,128)(2,1)S(1)}, bf16[128,128]{1,0:T(8,128)(2,1)S(1)}, bf16[128,128]{1,0:T(8,128)(2,1)S(1)}) custom-call(bf16[128,128]{1,0:T(8,128)(2,1)} %q_in.1, bf16[128,128]{1,0:T(8,128)(2,1)} %k_in.1, bf16[128,128]{1,0:T(8,128)(2,1)} %v_in.1, ...), custom_call_target="tpu_custom_call" | custom-call | tf_op jit(solution)/shard_map/pallas_call | solution.py:419
  20.1 0.7 %shard_map.129 = (bf16[128,128]{1,0:T(8,128)(2,1)}, bf16[128,128]{1,0:T(8,128)(2,1)}, bf16[128,128]{1,0:T(8,128)(2,1)}, bf16[128,128]{1,0:T(8,128)(2,1)}, bf16[128,128]{1,0:T(8,128)(2,1)}) custom-call(bf16[128,128]{1,0:T(8,128)(2,1)S(1)} %get-tuple-element.10.refs_0_, bf16[128,128]{1,0:T(8,128)(2,1)S(1)} %get-tuple-element.11.refs_1_, ...), custom_call_target="tpu_custom_call" | custom-call | tf_op jit(solution)/shard_map/pallas_call | solution.py:458
